TPU v7x, 1024 devices: a whole 4x4x32 slice. The times are simulated.
1024 devices in a mesh: section: 64 (over z, x_hi), dp: 16 (over y, x_lo, core).
Axes of the slice: x: 4 (x_hi: 2, x_lo: 2; x = x_hi * 2 + x_lo), y: 4, z: 32, core: 2. Of those that a mesh axis runs over, the one named last changes fastest.
Arguments:
- fwd_hidden: bfloat16 [64, 16, 64, 2048], P('section', 'dp'), may hold values from -6 to 6
- fwd_query: bfloat16 [64, 16, 64, 2048], P('section', 'dp'), may hold values from -32 to 32
- bwd_hidden: bfloat16 [64, 16, 64, 2048], P('section', 'dp'), may hold values from -6 to 6
- bwd_query: bfloat16 [64, 16, 64, 2048], P('section', 'dp'), may hold values from -32 to 32
- bwd_grad: bfloat16 [64, 16, 64, 2048], P('section', 'dp'), may hold values from -6 to 6
- prefix_keys: bfloat16 [64, 16, 2, 128, 512], P('section', 'dp'), may hold values from -6 to 6
- prefix_values: bfloat16 [64, 16, 2, 128, 512], P('section', 'dp'), may hold values from -6 to 6
- key_weight: bfloat16 [64, 2048, 512], P('section'), may hold values from -0.125 to 0.125
- value_weight: bfloat16 [64, 2048, 512], P('section'), may hold values from -0.125 to 0.125
- block_ids: int32 [64, 16, 2, 1], P('section', 'dp'), may hold values from 0 to 1, as said below
Outputs:
- next_hidden: bfloat16 [64, 16, 64, 2048], P('section', 'dp')
- prev_grad: bfloat16 [64, 16, 64, 2048], P('section', 'dp')
- query_grad: bfloat16 [64, 16, 64, 2048], P('section', 'dp')
- prefix_key_grad: bfloat16 [64, 16, 1, 128, 512], P('section', 'dp')
- prefix_value_grad: bfloat16 [64, 16, 1, 128, 512], P('section', 'dp')
- key_weight_grad: bfloat16 [64, 2048, 512], P('section', 'dp')
- value_weight_grad: bfloat16 [64, 2048, 512], P('section', 'dp')
Inputs may be any that keep to these rules, and one draw needn't show every extreme that they name: `block_ids`: the 1 indices of one group's list are distinct.
All inputs are finite; a program needn't handle non-finite values.
Results may differ from a plain program's by a relative error of at most 0.025.
Values may be sent and summed in bfloat16 or wider, within the bound.
No kernel may reach another device: no remote copies, remote signals or barrier semaphores. Data moves between devices by JAX's collectives and lax.ppermute only.
A program may use at most 64 MiB of HBM per device.

v0:
```python
import jax
import jax.numpy as jnp
from jax import lax
from jax.sharding import PartitionSpec as P

HEADS = 16
KVH = 4
HD = 128


def passed_along(value, axis, steps):
    count = lax.axis_size(axis)
    pairs = [(source, (source + steps) % count) for source in range(count)]
    return lax.ppermute(value, axis, pairs)


def from_behind(block, axis, distance):
    devices = range(lax.axis_size(axis))
    route = [(i - distance, i) for i in devices if i - distance in devices]
    return lax.ppermute(block, axis, route)


def kv_heads(hidden, weight_k, weight_v):
    keys_new = jnp.dot(hidden, weight_k, preferred_element_type=jnp.float32).astype(jnp.bfloat16)
    values_new = jnp.dot(hidden, weight_v, preferred_element_type=jnp.float32).astype(jnp.bfloat16)
    return (keys_new, values_new)


def gather_context(hidden, chosen_row, pool_keys, pool_values, weight_k, weight_v):
    keys_new, values_new = kv_heads(hidden, weight_k, weight_v)
    kv_width = pool_keys.shape[-1]
    prefix_keys_sel = jnp.take(pool_keys, chosen_row, axis=0).reshape(-1, kv_width)
    prefix_values_sel = jnp.take(pool_values, chosen_row, axis=0).reshape(-1, kv_width)
    keys_all = jnp.concatenate([prefix_keys_sel, keys_new], axis=0)
    values_all = jnp.concatenate([prefix_values_sel, values_new], axis=0)
    return (keys_all, values_all)


def softmax_probs(query_rows, keys_all, prefix_rows):
    row_count = query_rows.shape[0]
    key_count = keys_all.shape[0]
    query_heads = query_rows.reshape(row_count, KVH, HEADS // KVH, HD)
    key_heads = keys_all.reshape(key_count, KVH, HD)
    scores = jnp.einsum(
        "cgqd,kgd->gqck", query_heads, key_heads, preferred_element_type=jnp.float32
    ) * HD ** (-0.5)
    row_pos = jnp.arange(row_count)[:, None]
    col_pos = jnp.arange(key_count)[None, :]
    visible = (col_pos < prefix_rows) | (col_pos - prefix_rows <= row_pos)
    scores = jnp.where(visible, scores, -jnp.inf)
    highest = jnp.max(scores, axis=-1, keepdims=True)
    raised = jnp.exp(scores - highest)
    return raised / jnp.sum(raised, axis=-1, keepdims=True)


def per_device(
    fwd_hidden,
    fwd_query,
    bwd_hidden,
    bwd_query,
    bwd_grad,
    prefix_keys,
    prefix_values,
    key_weight,
    value_weight,
    block_ids,
):
    hidden_fwd = fwd_hidden[0, 0]
    query_fwd = fwd_query[0, 0]
    hidden_bwd = bwd_hidden[0, 0]
    query_bwd = bwd_query[0, 0]
    grad_out = bwd_grad[0, 0]
    pool_keys = prefix_keys[0, 0]
    pool_values = prefix_values[0, 0]
    weight_k = key_weight[0]
    weight_v = value_weight[0]
    chosen = block_ids[0, 0]
    row_count = hidden_fwd.shape[0]
    kv_width = pool_keys.shape[-1]
    prefix_rows = chosen.shape[1] * pool_keys.shape[1]
    keys_fwd, values_fwd = gather_context(
        hidden_fwd, chosen[0], pool_keys, pool_values, weight_k, weight_v
    )
    key_count = keys_fwd.shape[0]
    probs_fwd = softmax_probs(query_fwd, keys_fwd, prefix_rows)
    attended = jnp.einsum(
        "gqck,kgd->cgqd",
        probs_fwd.astype(jnp.bfloat16),
        values_fwd.reshape(key_count, KVH, HD),
        preferred_element_type=jnp.float32,
    ).reshape(row_count, -1)
    out_fwd = (hidden_fwd.astype(jnp.float32) + attended).astype(jnp.bfloat16)
    next_hidden = passed_along(out_fwd, "section", 1)
    keys_bwd, values_bwd = gather_context(
        hidden_bwd, chosen[1], pool_keys, pool_values, weight_k, weight_v
    )
    probs_bwd = softmax_probs(query_bwd, keys_bwd, prefix_rows)
    weights_bwd = probs_bwd.astype(jnp.bfloat16)
    grad_heads = grad_out.reshape(row_count, KVH, HEADS // KVH, HD)
    key_heads = keys_bwd.reshape(key_count, KVH, HD)
    value_heads = values_bwd.reshape(key_count, KVH, HD)
    query_heads = query_bwd.reshape(row_count, KVH, HEADS // KVH, HD)
    grad_probs = jnp.einsum(
        "cgqd,kgd->gqck", grad_heads, value_heads, preferred_element_type=jnp.float32
    )
    inner_sum = jnp.sum(probs_bwd * grad_probs, axis=-1, keepdims=True)
    grad_scores = (probs_bwd * (grad_probs - inner_sum) * HD ** (-0.5)).astype(jnp.bfloat16)
    query_grad = (
        jnp.einsum("gqck,kgd->cgqd", grad_scores, key_heads, preferred_element_type=jnp.float32)
        .reshape(row_count, -1)
        .astype(jnp.bfloat16)
    )
    key_grads = jnp.einsum(
        "gqck,cgqd->kgd", grad_scores, query_heads, preferred_element_type=jnp.float32
    ).reshape(key_count, kv_width)
    value_grads = jnp.einsum(
        "gqck,cgqd->kgd", weights_bwd, grad_heads, preferred_element_type=jnp.float32
    ).reshape(key_count, kv_width)
    prefix_key_grad = (
        key_grads[:prefix_rows]
        .astype(jnp.bfloat16)
        .reshape(chosen.shape[1], pool_keys.shape[1], kv_width)
    )
    prefix_value_grad = (
        value_grads[:prefix_rows]
        .astype(jnp.bfloat16)
        .reshape(chosen.shape[1], pool_keys.shape[1], kv_width)
    )
    own_keys = key_grads[prefix_rows:].astype(jnp.bfloat16)
    own_values = value_grads[prefix_rows:].astype(jnp.bfloat16)
    grad_back = (
        grad_out.astype(jnp.float32)
        + jnp.dot(own_keys, weight_k.T, preferred_element_type=jnp.float32)
        + jnp.dot(own_values, weight_v.T, preferred_element_type=jnp.float32)
    )
    prev_grad = from_behind(grad_back.astype(jnp.bfloat16), "section", -1)
    own_grads = jnp.concatenate([own_keys, own_values], axis=1)
    summed = lax.psum_scatter(
        jnp.einsum("cd,cj->dj", hidden_bwd, own_grads, preferred_element_type=jnp.float32).astype(
            jnp.bfloat16
        ),
        "dp",
        scatter_dimension=0,
        tiled=True,
    ).astype(jnp.float32)
    key_weight_grad = summed[:, :kv_width].astype(jnp.bfloat16)
    value_weight_grad = summed[:, kv_width:].astype(jnp.bfloat16)
    return (
        next_hidden[None, None],
        prev_grad[None, None],
        query_grad[None, None],
        prefix_key_grad[None, None],
        prefix_value_grad[None, None],
        key_weight_grad[None],
        value_weight_grad[None],
    )


def solution(mesh):
    return jax.shard_map(
        per_device,
        mesh=mesh,
        in_specs=(
            P("section", "dp", None, None),
            P("section", "dp", None, None),
            P("section", "dp", None, None),
            P("section", "dp", None, None),
            P("section", "dp", None, None),
            P("section", "dp", None, None, None),
            P("section", "dp", None, None, None),
            P("section", None, None),
            P("section", None, None),
            P("section", "dp", None, None),
        ),
        out_specs=(
            P("section", "dp", None, None),
            P("section", "dp", None, None),
            P("section", "dp", None, None),
            P("section", "dp", None, None, None),
            P("section", "dp", None, None, None),
            P("section", "dp", None),
            P("section", "dp", None),
        ),
        check_vma=False,
    )
```

profile of v0, /device:TPU:4, one launch (start us, length us, event | category | flops | bytes accessed | tf_op | source)
XLA Modules:
  0.0 159.8 jit_solution(2028565690259869807)
XLA Ops:
  8.4 1.3 fusion.109
  13.6 2.2 %fusion.45 = bf16[8,4,8,128]{3,2,1,0:T(8,128)(2,1)S(1)} fusion(bf16[1,2048,512]{2,1,0:T(8,128)(2,1)} %param.20, bf16[1,1,64,2048]{3,2,1,0:T(8,128)(2,1)} %param.14), kind=kOutput, calls=%fused_computation.43 | convolution fusion | flops 134250496 | bytes 2424832 | tf_op jit(solution)/shard_map/dot_general | solution.py:25
  17.6 0.9 reshape_squeeze.11
  18.5 0.9 reshape_squeeze.12
  20.6 0.8 copy.61
  22.1 1.3 convolution_bitcast_fusion
  23.4 3.0 %fusion.113 = (f32[4,4,64]{2,1,0:T(4,128)S(1)}, f32[4,4,64,192]{3,2,1,0:T(8,128)}) fusion(pred[64,192]{1,0:T(8,128)(4,1)S(1)} %fusion.85, bf16[64,4,4,128]{3,2,1,0:T(4,128)(2,1)} %reshape_squeeze.11, bf16[64,4,128]{2,0,1:T(8,128)(2,1)} %bitcast.194, bf16[128,4,128]{2,0,1:T(8,128)(2,1)} %copy.61), kind=kOutput, calls=%fused_computation.118 | convolution fusion | flops 51511488 | bytes 1261568 | tf_op jit(solution)/shard_map/sub | solution.py:52
  26.4 2.5 %convolution_bitcast_fusion.2 = bf16[192,4,128]{2,0,1:T(8,128)(2,1)} fusion(bf16[64,4,4,128]{3,2,1,0:T(4,128)(2,1)} %reshape_squeeze.12, f32[4,4,64,192]{3,2,1,0:T(8,128)} %get-tuple-element.49, f32[4,4,64]{2,1,0:T(4,128)S(1)} %get-tuple-element.48), kind=kOutput, calls=%fused_computation.34 | convolution fusion | flops 50724864 | bytes 1249280 | tf_op jit(solution)/shard_map/gqck,cgqd->kgd/dot_general | solution.py:116
  29.0 8.4 %convolution_bitcast_fusion.3 = bf16[192,4,128]{2,0,1:T(8,128)(2,1)} fusion(f32[4,4,64,192]{3,2,1,0:T(8,128)S(1)} %convolution_bitcast_fusion, bf16[64,4,4,128]{3,2,1,0:T(4,128)(2,1)} %reshape_squeeze.11, f32[4,4,64,192]{3,2,1,0:T(8,128)} %get-tuple-element.49, f32[4,4,64]{2,1,0:T(4,128)S(1)} %get-tuple-element.48), kind=kOutput, calls=%fused_computation.35 | convolution fusion | flops 51709120 | bytes 2035712 | tf_op jit(solution)/shard_map/gqck,cgqd->kgd/dot_general | solution.py:113
  37.4 0.8 copy_bitcast_fusion.1
  38.2 0.9 copy_bitcast_fusion
  39.1 3.3 %convert_bitcast_fusion = bf16[2048,1024]{0,1:T(8,128)(2,1)} fusion(bf16[1,1,64,2048]{3,2,1,0:T(8,128)(2,1)S(1)} %copy-done.2, bf16[64,512]{1,0:T(8,128)(2,1)S(1)} %copy_bitcast_fusion, bf16[64,512]{1,0:T(8,128)(2,1)S(1)} %copy_bitcast_fusion.1), kind=kOutput, calls=%fused_computation.3 | convolution fusion | flops 270794752 | bytes 4587520 | tf_op jit(solution)/shard_map/cd,cj->dj/dot_general | solution.py:139
  42.4 6.4 %copy.84 = bf16[2048,1024]{1,0:T(8,128)(2,1)} copy(bf16[2048,1024]{0,1:T(8,128)(2,1)} %convert_bitcast_fusion) | data formatting | bytes 8388608
  48.8 0.9 copy-done.3
  49.7 2.1 %fusion.48 = bf16[8,4,8,128]{3,2,1,0:T(8,128)(2,1)S(1)} fusion(bf16[1,2048,512]{2,1,0:T(8,128)(2,1)} %param.20, bf16[1,1,64,2048]{3,2,1,0:T(8,128)(2,1)S(1)} %copy-done.3), kind=kOutput, calls=%fused_computation.44 | convolution fusion | flops 134250496 | bytes 2424832 | tf_op jit(solution)/shard_map/dot_general | solution.py:25
  53.2 0.8 copy.54
  54.1 1.2 fusion.110
  55.3 1.3 fusion.24
  56.6 3.7 %convolution_bitcast_fusion.1 = f32[64,4,4,128]{3,0,2,1:T(8,128)} fusion(f32[4,4,64]{2,1,0:T(4,128)} %fusion.110, bf16[64,4,128]{2,0,1:T(8,128)(2,1)} %bitcast.196, bf16[128,4,128]{2,0,1:T(8,128)(2,1)} %copy.54, f32[4,4,64,192]{3,2,1,0:T(8,128)S(1)} %fusion.24), kind=kOutput, calls=%fused_computation.32 | convolution fusion | flops 51315904 | bytes 1511424 | tf_op jit(solution)/shard_map/gqck,kgd->cgqd/dot_general | solution.py:86
  60.3 1.4 copy.60
  62.7 3.9 %collective-permute-start = (bf16[64,2048]{1,0:T(8,128)(2,1)}, bf16[64,2048]{1,0:T(8,128)(2,1)S(1)}, u32[]{:S(2)}, u32[]{:S(2)}) collective-permute-start(bf16[64,2048]{1,0:T(8,128)(2,1)} %add_convert_fusion), channel_id=1, source_target_pairs={{0,16},{16,32},{32,48},{48,64},{64,80},{80,96},{96,112},{112,128},... | collective-permute-start | bytes 786440 | tf_op jit(solution)/shard_map/ppermute | solution.py:14
  66.6 1.7 %convolution_add_fusion.1 = f32[64,2048]{1,0:T(8,128)S(1)} fusion(bf16[1,2048,512]{2,1,0:T(8,128)(2,1)S(1)} %copy-done, bf16[1,1,64,2048]{3,2,1,0:T(8,128)(2,1)} %param.16, bf16[192,4,128]{2,0,1:T(8,128)(2,1)} %convolution_bitcast_fusion.3), kind=kOutput, calls=%fused_computation.5 | convolution fusion | flops 134479872 | bytes 2949120 | tf_op jit(solution)/shard_map/dot_general | solution.py:133
  69.1 13.4 %collective-permute-start.1 = (bf16[64,2048]{1,0:T(8,128)(2,1)S(1)}, bf16[64,2048]{1,0:T(8,128)(2,1)S(1)}, u32[]{:S(2)}, u32[]{:S(2)}) collective-permute-start(bf16[64,2048]{1,0:T(8,128)(2,1)S(1)} %fusion.3), channel_id=1, source_target_pairs={{16,0},{32,16},{48,32},{64,48},{80,64},{96,80},{112,96},{128,112},... | collective-permute-start | bytes 786440 | tf_op jit(solution)/shard_map/ppermute | solution.py:20
  82.6 8.5 %fusion.26 = bf16[64,4,4,128]{3,0,2,1:T(8,128)(2,1)} fusion(f32[4,4,64,192]{3,2,1,0:T(8,128)} %copy-done.5, bf16[64,4,128]{2,0,1:T(8,128)(2,1)S(1)} %bitcast.195, bf16[128,4,128]{2,0,1:T(8,128)(2,1)S(1)} %copy-done.15, f32[4,4,64,192]{3,2,1,0:T(8,128)} %get-tuple-element.49, f32[4,4,64]{2,1,0:T(4,128)S(1)} %copy-done.18), kind=kOutput, calls=%fused_computation.36 | convolution fusion | flops 52233408 | bytes 2035712 | tf_op jit(solution)/shard_map/gqck,kgd->cgqd/dot_general | solution.py:109
  91.0 1.2 copy.71
  92.2 0.9 convert_element_type.115
  93.2 0.8 copy.74
  94.1 0.8 copy.75
  94.9 53.9 %reduce-scatter.4.cloned.1.call-done = bf16[128,1024]{1,0:T(8,128)(2,1)} async-done(((bf16[2048,1024]{1,0:T(8,128)(2,1)}), bf16[128,1024]{1,0:T(8,128)(2,1)}) %reduce-scatter.4.cloned.1.call-update) | async-done | bytes 262160
  148.8 1.0 fusion.108
  149.9 0.8 copy.77
  150.8 0.8 copy.76
  (69 shorter events, 10.1 us)
Async XLA Ops:
  7.2 9.3 %copy-start = (bf16[1,2048,512]{2,1,0:T(8,128)(2,1)S(1)}, bf16[1,2048,512]{2,1,0:T(8,128)(2,1)}, u32[]{:S(2)}) copy-start(bf16[1,2048,512]{2,1,0:T(8,128)(2,1)} %param.19) | copy-start | bytes 6291460
  7.2 9.3 %copy-start.2 = (bf16[1,1,64,2048]{3,2,1,0:T(8,128)(2,1)S(1)}, bf16[1,1,64,2048]{3,2,1,0:T(8,128)(2,1)}, u32[]{:S(2)}) copy-start(bf16[1,1,64,2048]{3,2,1,0:T(8,128)(2,1)} %param.14) | copy-start | bytes 786436
  7.2 141.6 %reduce-scatter.4.cloned.1.call-start = ((), (), s32[]{:S(2)}) async-start(), calls=%async_computation.1 | async-start | bytes 4456448
  13.6 4.0 %copy-start.11 = (bf16[1,1,64,2048]{3,2,1,0:T(8,128)(2,1)S(1)}, bf16[1,1,64,2048]{3,2,1,0:T(8,128)(2,1)}, u32[]{:S(2)}) copy-start(bf16[1,1,64,2048]{3,2,1,0:T(8,128)(2,1)} %param.15) | copy-start | bytes 786436
  15.8 2.7 %copy-start.4 = (bf16[1,1,64,2048]{3,2,1,0:T(8,128)(2,1)S(1)}, bf16[1,1,64,2048]{3,2,1,0:T(8,128)(2,1)}, u32[]{:S(2)}) copy-start(bf16[1,1,64,2048]{3,2,1,0:T(8,128)(2,1)} %param.16) | copy-start | bytes 786436
  15.8 3.5 %copy-start.12 = (bf16[1,1,2,128,512]{4,3,2,1,0:T(8,128)(2,1)S(1)}, bf16[1,1,2,128,512]{4,3,2,1,0:T(8,128)(2,1)}, u32[]{:S(2)}) copy-start(bf16[1,1,2,128,512]{4,3,2,1,0:T(8,128)(2,1)} %param.17) | copy-start | bytes 786436
  16.5 3.1 %copy-start.13 = (bf16[1,1,2,128,512]{4,3,2,1,0:T(8,128)(2,1)S(1)}, bf16[1,1,2,128,512]{4,3,2,1,0:T(8,128)(2,1)}, u32[]{:S(2)}) copy-start(bf16[1,1,2,128,512]{4,3,2,1,0:T(8,128)(2,1)} %param.18) | copy-start | bytes 786436
  23.4 5.5 %copy-start.5 = (f32[4,4,64,192]{3,2,1,0:T(8,128)}, f32[4,4,64,192]{3,2,1,0:T(8,128)S(1)}, u32[]{:S(2)}) copy-start(f32[4,4,64,192]{3,2,1,0:T(8,128)S(1)} %convolution_bitcast_fusion) | copy-start | bytes 2359300
  26.4 2.5 %copy-start.17 = (f32[4,4,64]{2,1,0:T(4,128)}, f32[4,4,64]{2,1,0:T(4,128)S(1)}, u32[]{:S(2)}) copy-start(f32[4,4,64]{2,1,0:T(4,128)S(1)} %get-tuple-element.48) | copy-start | bytes 12292
  48.8 0.9 copy-start.3
  49.7 3.3 %copy-start.14 = (bf16[1,1,64,2048]{3,2,1,0:T(8,128)(2,1)S(1)}, bf16[1,1,64,2048]{3,2,1,0:T(8,128)(2,1)}, u32[]{:S(2)}) copy-start(bf16[1,1,64,2048]{3,2,1,0:T(8,128)(2,1)} %param.13) | copy-start | bytes 786436
  51.8 1.4 copy-start.9
  51.8 2.1 %copy-start.8 = (bf16[1,128,512]{1,2,0:T(8,128)(2,1)S(1)}, bf16[1,128,512]{1,2,0:T(8,128)(2,1)}, u32[]{:S(2)}) copy-start(bf16[1,128,512]{1,2,0:T(8,128)(2,1)} %get-tuple-element.50) | copy-start | bytes 393220
  53.0 1.1 copy-start.10
  53.2 0.9 copy-start.6
  61.9 6.4 %copy-start.1 = (bf16[1,2048,512]{2,1,0:T(8,128)(2,1)S(1)}, bf16[1,2048,512]{2,1,0:T(8,128)(2,1)}, u32[]{:S(2)}) copy-start(bf16[1,2048,512]{2,1,0:T(8,128)(2,1)} %param.20) | copy-start | bytes 6291460
  61.9 6.4 %copy-start.7 = (bf16[192,4,128]{2,0,1:T(8,128)(2,1)S(1)}, bf16[192,4,128]{2,0,1:T(8,128)(2,1)}, u32[]{:S(2)}) copy-start(bf16[192,4,128]{2,0,1:T(8,128)(2,1)} %convolution_bitcast_fusion.2) | copy-start | bytes 589828
  62.7 32.2 %collective-permute-start = (bf16[64,2048]{1,0:T(8,128)(2,1)}, bf16[64,2048]{1,0:T(8,128)(2,1)S(1)}, u32[]{:S(2)}, u32[]{:S(2)}) collective-permute-start(bf16[64,2048]{1,0:T(8,128)(2,1)} %add_convert_fusion), channel_id=1, source_target_pairs={{0,16},{16,32},{32,48},{48,64},{64,80},{80,96},{96,112},{112,128},... | collective-permute-start | bytes 786440 | tf_op jit(solution)/shard_map/ppermute | solution.py:14
  68.3 14.2 %copy-start.15 = (bf16[128,4,128]{2,0,1:T(8,128)(2,1)S(1)}, bf16[128,4,128]{2,0,1:T(8,128)(2,1)}, u32[]{:S(2)}) copy-start(bf16[128,4,128]{2,0,1:T(8,128)(2,1)} %copy.61) | copy-start | bytes 393220
  68.4 14.2 %copy-start.16 = (bf16[8,4,8,128]{3,2,0,1:T(8,128)(2,1)S(1)}, bf16[8,4,8,128]{3,2,0,1:T(8,128)(2,1)}, u32[]{:S(2)}) copy-start(bf16[8,4,8,128]{3,2,0,1:T(8,128)(2,1)} %copy.123) | copy-start | bytes 196612
  68.4 14.2 %copy-start.18 = (f32[4,4,64]{2,1,0:T(4,128)S(1)}, f32[4,4,64]{2,1,0:T(4,128)}, u32[]{:S(2)}) copy-start(f32[4,4,64]{2,1,0:T(4,128)} %copy-done.17) | copy-start | bytes 12292
  69.1 25.8 %collective-permute-start.1 = (bf16[64,2048]{1,0:T(8,128)(2,1)S(1)}, bf16[64,2048]{1,0:T(8,128)(2,1)S(1)}, u32[]{:S(2)}, u32[]{:S(2)}) collective-permute-start(bf16[64,2048]{1,0:T(8,128)(2,1)S(1)} %fusion.3), channel_id=1, source_target_pairs={{16,0},{32,16},{48,32},{64,48},{80,64},{96,80},{112,96},{128,112},... | collective-permute-start | bytes 786440 | tf_op jit(solution)/shard_map/ppermute | solution.py:20
  82.6 10.5 %slice-start.1 = ((bf16[192,4,128]{2,0,1:T(8,128)(2,1)}), bf16[128,4,128]{2,0,1:T(8,128)(2,1)S(1)}, s32[]{:S(2)}) async-start(bf16[192,4,128]{2,0,1:T(8,128)(2,1)} %convolution_bitcast_fusion.3), calls=%async_computation.3 | async-start | bytes 262144 | tf_op jit(solution)/shard_map/slice | solution.py:120
  82.6 11.4 %slice-start = ((bf16[192,4,128]{2,0,1:T(8,128)(2,1)}), bf16[128,4,128]{2,0,1:T(8,128)(2,1)S(1)}, s32[]{:S(2)}) async-start(bf16[192,4,128]{2,0,1:T(8,128)(2,1)} %convolution_bitcast_fusion.2), calls=%async_computation.2 | async-start | bytes 262144 | tf_op jit(solution)/shard_map/slice | solution.py:125
Sparse Core Ops, SparseCore 0:
  48.9 99.8 reduce-scatter.3
where the time goes:
time: 161 us; the launch traced here: 160 us
  waiting for transfers between devices  53.9 us (33%)
  matrix products  40.9 us (25%)
  local copies, waits for them, and re-layouts  26.1 us (16%)
  between operations  18.3 us (11%)
  starting transfers between devices  17.3 us (11%)
  other arithmetic  3.35 us (2%)
    unnamed x2, waiting for transfers between devices  53.9 us
    ppermute x1, starting transfers between devices, from_behind(): return lax.ppermute(block, axis, route)  13.4 us
    unnamed x49, local copies, waits for them, and re-layouts  12.5 us
    dot_general x1, matrix products, per_device(): jnp.einsum('gqck,kgd->cgqd', grad_scores, key_heads, preferred_element_ty...  8.45 us
    dot_general x1, matrix products, per_device(): jnp.einsum('gqck,cgqd->kgd', grad_scores, query_heads, preferred_element_...  8.42 us
    dot_general x2, matrix products, kv_heads(): jnp.dot(hidden, weight_v, preferred_element_type=jnp.float32)  4.31 us
    sub x2, matrix products, softmax_probs(): raised = jnp.exp(scores - highest)  4.17 us
    ppermute x1, starting transfers between devices, passed_along(): return lax.ppermute(value, axis, pairs)  3.88 us
  transfers between devices with their start and end apart: 3, of which 1 were waited for; matrix products, arithmetic and copies ran while one was open for 17% of the time, Pallas kernels for 0%

commit v1 on v0

v1 whole, which is shorter than its diff:
```python
import functools

import jax
import jax.numpy as jnp
from jax import lax
from jax.experimental import pallas as pl
from jax.experimental.pallas import tpu as pltpu
from jax.sharding import PartitionSpec as P

HEADS = 16
KVH = 4
HD = 128
GROUP = HEADS // KVH
D = 2048
CH = 64
BLK = 128
KVW = KVH * HD
KEYS = BLK + CH
SCALE = HD ** (-0.5)
CHIPS = 8
ROWS = D // CHIPS
HALF = ROWS // 2
CHUNKS = 4
STEP = D // CHUNKS
F32 = jnp.float32
BF16 = jnp.bfloat16

VMEM = pltpu.VMEM
ANY = pl.ANY
SMEM = pltpu.SMEM


def nt(a, b):
    return lax.dot_general(a, b, (((1,), (1,)), ((), ())), preferred_element_type=F32)


def nn(a, b):
    return lax.dot_general(a, b, (((1,), (0,)), ((), ())), preferred_element_type=F32)


def tn(a, b):
    return lax.dot_general(a, b, (((0,), (0,)), ((), ())), preferred_element_type=F32)


def stacked(ref, g):
    return jnp.concatenate(
        [ref[:, (g * GROUP + j) * HD : (g * GROUP + j + 1) * HD] for j in range(GROUP)], axis=0
    )


def probs_t(keys, query):
    score = nt(keys, query) * SCALE
    key_at = lax.broadcasted_iota(jnp.int32, (CH, GROUP * CH), 0)
    row_at = lax.broadcasted_iota(jnp.int32, (CH, GROUP * CH), 1) % CH
    own = jnp.where(key_at <= row_at, score[BLK:], -jnp.inf)
    score = jnp.concatenate([score[:BLK], own], axis=0)
    raised = jnp.exp(score - jnp.max(score, axis=0, keepdims=True))
    return raised * (1.0 / jnp.sum(raised, axis=0, keepdims=True))


def project(hid, weight, parts, wait):
    total = None
    for c in parts:
        wait(c)
        part = nn(hid[:, c * STEP : (c + 1) * STEP], weight[c * STEP : (c + 1) * STEP, :])
        total = part if total is None else total + part
    return total.astype(BF16)


def backward_kernel(
    ids, hid_h, q_h, g_h, pk_h, pv_h, wk_h, wv_h,
    send_h, own_h, pkg_h, pvg_h, gs_h, keys_h,
    hid, q, g, keys, values, wk, wv, own, pkg, pvg, gs, sem, wsem, osem,
):
    block = ids[1]
    load = [
        pltpu.make_async_copy(hid_h, hid, sem.at[0]),
        pltpu.make_async_copy(q_h, q, sem.at[1]),
        pltpu.make_async_copy(pk_h.at[block], keys.at[pl.ds(0, BLK)], sem.at[2]),
        pltpu.make_async_copy(g_h, g, sem.at[3]),
        pltpu.make_async_copy(pv_h.at[block], values.at[pl.ds(0, BLK)], sem.at[4]),
    ]
    wload = []
    for i, (src, dst) in enumerate(((wk_h, wk), (wv_h, wv))):
        for c in range(CHUNKS):
            at = pl.ds(c * STEP, STEP)
            wload.append(pltpu.make_async_copy(src.at[at], dst.at[at], wsem.at[i * CHUNKS + c]))
    load[0].start()
    for copy in wload[:CHUNKS]:
        copy.start()
    for copy in load[1:3]:
        copy.start()
    for copy in wload[CHUNKS:]:
        copy.start()
    for copy in load[3:]:
        copy.start()
    load[0].wait()
    out = []

    def put(src, dst):
        copy = pltpu.make_async_copy(src, dst, osem.at[len(out)])
        copy.start()
        out.append(copy)

    for t in range(CHIPS):
        put(hid.at[:, pl.ds(t * ROWS, ROWS)], send_h.at[t, :, pl.ds(0, ROWS)])
    keys[BLK:, :] = project(hid, wk, range(CHUNKS), lambda c: wload[c].wait())
    values[BLK:, :] = project(hid, wv, range(CHUNKS), lambda c: wload[CHUNKS + c].wait())
    for copy in load[1:]:
        copy.wait()
    put(keys, keys_h)
    for h in range(KVH):
        at = slice(h * HD, (h + 1) * HD)
        query, grad = stacked(q, h), stacked(g, h)
        probs = probs_t(keys[:, at], query)
        grad_probs = nt(values[:, at], grad)
        inner = jnp.sum(probs * grad_probs, axis=0, keepdims=True)
        grad_scores = (probs * (grad_probs - inner) * SCALE).astype(BF16)
        gs[h] = grad_scores
        key_grads = nn(grad_scores, query)
        value_grads = nn(probs.astype(BF16), grad)
        own[:, at] = key_grads[BLK:].astype(BF16)
        own[:, KVW + h * HD : KVW + (h + 1) * HD] = value_grads[BLK:].astype(BF16)
        pkg[:, at] = key_grads[:BLK].astype(BF16)
        pvg[:, at] = value_grads[:BLK].astype(BF16)
    for t in range(CHIPS):
        put(own, send_h.at[t, :, pl.ds(ROWS, 2 * KVW)])
    put(own, own_h)
    put(pkg, pkg_h)
    put(pvg, pvg_h)
    put(gs, gs_h)
    for copy in out:
        copy.wait()


def forward_kernel(
    ids, hid_h, q_h, pk_h, pv_h, wk_h, wv_h, g_h, own_h,
    fwd_h, back_h,
    hid, q, keys, values, wk, wv, g, own, fwd, back, sem, wsem, osem,
):
    block = ids[0]
    load = [
        pltpu.make_async_copy(g_h, g, sem.at[0]),
        pltpu.make_async_copy(own_h, own, sem.at[1]),
        pltpu.make_async_copy(hid_h, hid, sem.at[2]),
        pltpu.make_async_copy(q_h, q, sem.at[3]),
        pltpu.make_async_copy(pk_h.at[block], keys.at[pl.ds(0, BLK)], sem.at[4]),
        pltpu.make_async_copy(pv_h.at[block], values.at[pl.ds(0, BLK)], sem.at[5]),
    ]
    wload = []
    for i, (src, dst) in enumerate(((wk_h, wk), (wv_h, wv))):
        for c in range(CHUNKS):
            at = pl.ds(c * STEP, STEP)
            wload.append(pltpu.make_async_copy(src.at[at], dst.at[at], wsem.at[i * CHUNKS + c]))
    for copy in load[:3]:
        copy.start()
    for c in range(CHUNKS):
        wload[c].start()
        wload[CHUNKS + c].start()
    for copy in load[3:]:
        copy.start()
    for copy in load[:3]:
        copy.wait()
    key_total = value_total = None
    for c in range(CHUNKS):
        at = slice(c * STEP, (c + 1) * STEP)
        wload[c].wait()
        wload[CHUNKS + c].wait()
        back[:, at] = (
            g[:, at].astype(F32)
            + nt(own[:, :KVW], wk[at, :])
            + nt(own[:, KVW:], wv[at, :])
        ).astype(BF16)
        key_part = nn(hid[:, at], wk[at, :])
        value_part = nn(hid[:, at], wv[at, :])
        key_total = key_part if c == 0 else key_total + key_part
        value_total = value_part if c == 0 else value_total + value_part
    back_out = pltpu.make_async_copy(back, back_h, osem.at[0])
    back_out.start()
    keys[BLK:, :] = key_total.astype(BF16)
    values[BLK:, :] = value_total.astype(BF16)
    for copy in load[3:]:
        copy.wait()
    for h in range(KVH):
        at = slice(h * HD, (h + 1) * HD)
        weights = probs_t(keys[:, at], stacked(q, h)).astype(BF16)
        attended = tn(weights, values[:, at])
        for j in range(GROUP):
            cols = slice((h * GROUP + j) * HD, (h * GROUP + j + 1) * HD)
            fwd[:, cols] = (
                hid[:, cols].astype(F32) + attended[j * CH : (j + 1) * CH]
            ).astype(BF16)
    fwd_out = pltpu.make_async_copy(fwd, fwd_h, osem.at[1])
    fwd_out.start()
    back_out.wait()
    fwd_out.wait()


def query_kernel(gs, keys, out):
    for h in range(KVH):
        grad = tn(gs[h], keys[:, h * HD : (h + 1) * HD])
        for j in range(GROUP):
            cols = slice((h * GROUP + j) * HD, (h * GROUP + j + 1) * HD)
            out[:, cols] = grad[j * CH : (j + 1) * CH].astype(BF16)


def weight_kernel(core, recv, mine, theirs):
    here = core[0]
    grads = recv[:, :, ROWS:].reshape(CHIPS * CH, 2 * KVW)
    low = tn(recv[:, :, :HALF].reshape(CHIPS * CH, HALF), grads)
    high = tn(recv[:, :, HALF:ROWS].reshape(CHIPS * CH, HALF), grads)
    first = here == 0
    mine[...] = jnp.where(first, low, high)
    theirs[...] = jnp.where(first, high, low).astype(BF16)


def sum_kernel(core, mine, both, key_grad, value_grad):
    other = both[1 - core[0]].astype(F32)
    key_grad[...] = (mine[:, :KVW] + other[:, :KVW]).astype(BF16)
    value_grad[...] = (mine[:, KVW:] + other[:, KVW:]).astype(BF16)


def call(kernel, outs, scratch, flops, in_specs, out_specs, size=62):
    return pl.pallas_call(
        kernel,
        out_shape=[jax.ShapeDtypeStruct(s, t) for s, t in outs],
        in_specs=in_specs,
        out_specs=out_specs,
        scratch_shapes=scratch,
        compiler_params=pltpu.CompilerParams(vmem_limit_bytes=size * 1024 * 1024),
        cost_estimate=pl.CostEstimate(flops=flops, bytes_accessed=6 << 20, transcendentals=200000),
    )


def spec(space):
    return pl.BlockSpec(memory_space=space)


def along(value, axis, steps, wrap):
    count = lax.axis_size(axis)
    pairs = [(i, (i + steps) % count) for i in range(count) if wrap or 0 <= i + steps < count]
    return lax.ppermute(value, axis, pairs)


def per_device(
    fwd_hidden, fwd_query, bwd_hidden, bwd_query, bwd_grad,
    prefix_keys, prefix_values, key_weight, value_weight, block_ids,
):
    count = lax.axis_size("dp")
    dma = pltpu.SemaphoreType.DMA
    wide, kv, weight = (CH, D), (KEYS, KVW), (D, KVW)
    pool_keys, pool_values = prefix_keys[0, 0], prefix_values[0, 0]
    weight_k, weight_v = key_weight[0], value_weight[0]
    grad = bwd_grad[0, 0]
    ids = block_ids.reshape(2)
    send, own, pkg, pvg, gs, keys_bwd = call(
        backward_kernel,
        [
            ((CHIPS, CH, ROWS + 2 * KVW), BF16),
            ((CH, 2 * KVW), BF16),
            ((BLK, KVW), BF16),
            ((BLK, KVW), BF16),
            ((KVH, KEYS, GROUP * CH), BF16),
            (kv, BF16),
        ],
        [VMEM(wide, BF16)] * 3
        + [VMEM(kv, BF16)] * 2
        + [VMEM(weight, BF16)] * 2
        + [VMEM((CH, 2 * KVW), BF16)]
        + [VMEM((BLK, KVW), BF16)] * 2
        + [VMEM((KVH, KEYS, GROUP * CH), BF16), dma((5,)), dma((2 * CHUNKS,)), dma((24,))],
        800_000_000,
        [spec(SMEM)] + [spec(ANY)] * 7,
        [spec(ANY)] * 6,
    )(ids, bwd_hidden[0, 0], bwd_query[0, 0], grad, pool_keys, pool_values, weight_k, weight_v)
    same_core = [[2 * t + c for t in range(count // 2)] for c in range(2)]
    pairs = [[2 * t, 2 * t + 1] for t in range(count // 2)]
    recv = lax.all_to_all(send, "dp", 0, 0, tiled=True, axis_index_groups=same_core)
    out_fwd, out_bwd = call(
        forward_kernel,
        [(wide, BF16), (wide, BF16)],
        [VMEM(wide, BF16)] * 2
        + [VMEM(kv, BF16)] * 2
        + [VMEM(weight, BF16)] * 2
        + [VMEM(wide, BF16), VMEM((CH, 2 * KVW), BF16)]
        + [VMEM(wide, BF16)] * 2
        + [dma((6,)), dma((2 * CHUNKS,)), dma((2,))],
        800_000_000,
        [spec(SMEM)] + [spec(ANY)] * 8,
        [spec(ANY)] * 2,
    )(
        ids, fwd_hidden[0, 0], fwd_query[0, 0], pool_keys, pool_values,
        weight_k, weight_v, grad, own,
    )
    next_hidden = along(out_fwd, "section", 1, True)
    prev_grad = along(out_bwd, "section", -1, False)
    (query_grad,) = call(
        query_kernel,
        [(wide, BF16)],
        [],
        100_000_000,
        [spec(VMEM)] * 2,
        [spec(VMEM)],
        16,
    )(gs, keys_bwd)
    core = lax.axis_index("dp") & 1
    mine, theirs = call(
        weight_kernel,
        [((HALF, 2 * KVW), F32), ((HALF, 2 * KVW), BF16)],
        [],
        270_000_000,
        [spec(SMEM), spec(VMEM)],
        [spec(VMEM)] * 2,
        16,
    )(core.reshape(1), recv)
    both = lax.all_gather(theirs, "dp", axis=0, axis_index_groups=pairs)
    key_weight_grad, value_weight_grad = call(
        sum_kernel,
        [((HALF, KVW), BF16)] * 2,
        [],
        1_000_000,
        [spec(SMEM)] + [spec(VMEM)] * 2,
        [spec(VMEM)] * 2,
        16,
    )(core.reshape(1), mine, both)
    return (
        next_hidden[None, None],
        prev_grad[None, None],
        query_grad[None, None],
        pkg[None, None, None],
        pvg[None, None, None],
        key_weight_grad[None],
        value_weight_grad[None],
    )


def solution(mesh):
    device = P("section", "dp")
    return jax.shard_map(
        per_device,
        mesh=mesh,
        in_specs=(device,) * 7 + (P("section"),) * 2 + (device,),
        out_specs=(device,) * 5 + (P("section", "dp"),) * 2,
        check_vma=False,
    )
```

time: 161 us -> 53.4 us (0.33)
  the two profiles are of different devices: /device:TPU:4 before, /device:TPU:1 now
where the time goes in v1:
time: 53.4 us; the launch traced here: 53.1 us
  waiting for transfers between devices  19.8 us (37%)
  Pallas kernels  15 us (28%)
  starting transfers between devices  11.6 us (22%)
  blocking collectives  4.59 us (9%)
  local copies, waits for them, and re-layouts  1.41 us (3%)
  between operations  0.71 us (1%)
    ppermute x2, waiting for transfers between devices, along(): return lax.ppermute(value, axis, pairs)  19.8 us
    pallas_call x1, Pallas kernels, per_device(): call(backward_kernel, [((CHIPS, CH, ROWS + 2 * KVW), BF16), ((CH, 2 * KVW...  6.43 us
    pallas_call x1, Pallas kernels, per_device(): call(forward_kernel, [(wide, BF16), (wide, BF16)], [VMEM(wide, BF16)] * 2...  6.32 us
    all_to_all x1, starting transfers between devices, per_device(): lax.all_to_all(send, 'dp', 0, 0, tiled=True, axis_index_groups=same_core)  5.96 us
    ppermute x2, starting transfers between devices, along(): return lax.ppermute(value, axis, pairs)  5.65 us
    all_gather x1, blocking collectives, per_device(): both = lax.all_gather(theirs, 'dp', axis=0, axis_index_groups=pairs)  4.59 us
    unnamed x6, local copies, waits for them, and re-layouts  1.41 us
  transfers between devices with their start and end apart: 3, of which 1 were waited for; matrix products, arithmetic and copies ran while one was open for 0% of the time, Pallas kernels for 14%

profile of v1, /device:TPU:1, one launch (start us, length us, event | category | flops | bytes accessed | tf_op | source)
XLA Modules:
  0.0 53.1 jit_solution(1800239040958286350)
XLA Ops:
  0.6 6.4 %shard_map.153 = (bf16[8,64,1280]{2,1,0:T(8,128)(2,1)}, bf16[64,1024]{1,0:T(8,128)(2,1)}, bf16[128,512]{1,0:T(8,128)(2,1)}, bf16[128,512]{1,0:T(8,128)(2,1)}, bf...) custom-call(s32[2]{0:T(128)} %bitcast.37, bf16[64,2048]{1,0:T(8,128)(2,1)} %bitcast.30, bf16[64,2048]{1,0:T(8,128)(2,1)} %bitcast.31, ...), custom_call_target="tpu_custom_call" | custom-call | flops 800000000 | bytes 6291456 | tf_op jit(solution)/shard_map/pallas_call | solution.py:256
  7.1 6.0 %all-to-all-start = ((bf16[8,64,1280]{2,1,0:T(8,128)(2,1)}), bf16[8,64,1280]{2,1,0:T(8,128)(2,1)S(1)}, u32[]{:S(2)}, u32[]{:S(2)}) async-start(bf16[8,64,1280]{2,1,0:T(8,128)(2,1)} %get-tuple-element.26), calls=%async_computation | async-start | bytes 2621440 | tf_op jit(solution)/shard_map/all_to_all | solution.py:278
  13.0 0.0 copy-start
  13.0 0.0 copy-start.1
  13.0 6.3 %shard_map.154 = (bf16[64,2048]{1,0:T(8,128)(2,1)}, bf16[64,2048]{1,0:T(8,128)(2,1)}) custom-call(s32[2]{0:T(128)} %bitcast.38, bf16[64,2048]{1,0:T(8,128)(2,1)} %bitcast.32, bf16[64,2048]{1,0:T(8,128)(2,1)} %bitcast.33, bf16[2,128,512]{2,1,0:T(8,128)(2,1)} %bitcast.25, bf16[2,128,512]{2,1,0:T(8,128)(2,1)} %bitcast.27, bf16[2048,512]{1,0:T(8,128)(2,1)} %bitcast.21, ...), custom_call_target="tpu_custom_call" | custom-call | flops 800000000 | bytes 6291456 | tf_op jit(solution)/shard_map/pallas_call | solution.py:279
  19.4 4.4 %collective-permute-start = (bf16[64,2048]{1,0:T(8,128)(2,1)}, bf16[64,2048]{1,0:T(8,128)(2,1)S(1)}, u32[]{:S(2)}, u32[]{:S(2)}) collective-permute-start(bf16[64,2048]{1,0:T(8,128)(2,1)} %get-tuple-element.20), channel_id=1, source_target_pairs={{0,16},{16,32},{32,48},{48,64},{64,80},{80,96},{96,112},{112,128},... | collective-permute-start | bytes 786440 | tf_op jit(solution)/shard_map/ppermute | solution.py:242
  23.7 1.3 %collective-permute-start.1 = (bf16[64,2048]{1,0:T(8,128)(2,1)}, bf16[64,2048]{1,0:T(8,128)(2,1)S(1)}, u32[]{:S(2)}, u32[]{:S(2)}) collective-permute-start(bf16[64,2048]{1,0:T(8,128)(2,1)} %get-tuple-element.21), channel_id=1, source_target_pairs={{16,0},{32,16},{48,32},{64,48},{80,64},{96,80},{112,96},{128,112},... | collective-permute-start | bytes 786440 | tf_op jit(solution)/shard_map/ppermute | solution.py:242
  25.0 0.0 copy-done
  25.1 0.0 copy-done.1
  25.1 1.1 %shard_map.155 = bf16[64,2048]{1,0:T(8,128)(2,1)} custom-call(bf16[4,192,256]{2,1,0:T(8,128)(2,1)S(1)} %copy-done, bf16[192,512]{1,0:T(8,128)(2,1)S(1)} %copy-done.1), custom_call_target="tpu_custom_call" | custom-call | flops 100000000 | bytes 6291456 | tf_op jit(solution)/shard_map/pallas_call | solution.py:297
  26.1 19.8 %collective-permute-done = bf16[64,2048]{1,0:T(8,128)(2,1)S(1)} collective-permute-done((bf16[64,2048]{1,0:T(8,128)(2,1)}, bf16[64,2048]{1,0:T(8,128)(2,1)S(1)}, u32[]{:S(2)}, u32[]{:S(2)}) %collective-permute-start) | collective-permute-done | bytes 262176 | tf_op jit(solution)/shard_map/ppermute | solution.py:242
  45.9 0.0 collective-permute-done.1
  45.9 0.0 all-to-all-done.recv
  45.9 0.5 shard_map.156
  46.4 4.6 %all-gather = bf16[256,1024]{1,0:T(8,128)(2,1)S(1)} all-gather(bf16[128,1024]{1,0:T(8,128)(2,1)S(1)} %get-tuple-element.28), channel_id=2, replica_groups={{0,1},{2,3},{4,5},{6,7},{8,9},{10,11},{12,13},{14,15},{16,17},{18,19},{..., dimensions={0}, use_global_device_ids=true | all-gather | bytes 786432 | tf_op jit(solution)/shard_map/all_gather | solution.py:316
  51.0 0.7 %shard_map.157 = (bf16[128,512]{1,0:T(8,128)(2,1)}, bf16[128,512]{1,0:T(8,128)(2,1)}) custom-call(s32[1]{0:T(128)} %bitcast.15.core, f32[128,1024]{1,0:T(8,128)S(1)} %get-tuple-element.27.mine, bf16[2,128,1024]{2,1,0:T(8,128)(2,1)S(1)} %bitcast.19), custom_call_target="tpu_custom_call" | custom-call | flops 1000000 | bytes 6291456 | tf_op jit(solution)/shard_map/pallas_call | solution.py:317
  51.7 0.7 %copy.19 = bf16[1,1,64,2048]{3,2,1,0:T(8,128)(2,1)} copy(bf16[1,1,64,2048]{3,2,1,0:T(8,128)(2,1)S(1)} %bitcast.35) | data formatting | bytes 524288
  52.4 0.7 %copy.20 = bf16[1,1,64,2048]{3,2,1,0:T(8,128)(2,1)} copy(bf16[1,1,64,2048]{3,2,1,0:T(8,128)(2,1)S(1)} %bitcast.36) | data formatting | bytes 524288
Async XLA Ops:
  7.1 38.8 %all-to-all-start = ((bf16[8,64,1280]{2,1,0:T(8,128)(2,1)}), bf16[8,64,1280]{2,1,0:T(8,128)(2,1)S(1)}, u32[]{:S(2)}, u32[]{:S(2)}) async-start(bf16[8,64,1280]{2,1,0:T(8,128)(2,1)} %get-tuple-element.26), calls=%async_computation | async-start | bytes 2621440 | tf_op jit(solution)/shard_map/all_to_all | solution.py:278
  13.0 12.0 %copy-start = (bf16[4,192,256]{2,1,0:T(8,128)(2,1)S(1)}, bf16[4,192,256]{2,1,0:T(8,128)(2,1)}, u32[]{:S(2)}) copy-start(bf16[4,192,256]{2,1,0:T(8,128)(2,1)} %get-tuple-element.22.gs) | copy-start | bytes 1179652
  13.0 12.0 %copy-start.1 = (bf16[192,512]{1,0:T(8,128)(2,1)S(1)}, bf16[192,512]{1,0:T(8,128)(2,1)}, u32[]{:S(2)}) copy-start(bf16[192,512]{1,0:T(8,128)(2,1)} %get-tuple-element.23.keys) | copy-start | bytes 589828
  19.4 26.5 %collective-permute-start = (bf16[64,2048]{1,0:T(8,128)(2,1)}, bf16[64,2048]{1,0:T(8,128)(2,1)S(1)}, u32[]{:S(2)}, u32[]{:S(2)}) collective-permute-start(bf16[64,2048]{1,0:T(8,128)(2,1)} %get-tuple-element.20), channel_id=1, source_target_pairs={{0,16},{16,32},{32,48},{48,64},{64,80},{80,96},{96,112},{112,128},... | collective-permute-start | bytes 786440 | tf_op jit(solution)/shard_map/ppermute | solution.py:242
  23.7 22.2 %collective-permute-start.1 = (bf16[64,2048]{1,0:T(8,128)(2,1)}, bf16[64,2048]{1,0:T(8,128)(2,1)S(1)}, u32[]{:S(2)}, u32[]{:S(2)}) collective-permute-start(bf16[64,2048]{1,0:T(8,128)(2,1)} %get-tuple-element.21), channel_id=1, source_target_pairs={{16,0},{32,16},{48,32},{64,48},{80,64},{96,80},{112,96},{128,112},... | collective-permute-start | bytes 786440 | tf_op jit(solution)/shard_map/ppermute | solution.py:242

commit v2 on v1

v2 whole, which is shorter than its diff:
```python
import functools

import jax
import jax.numpy as jnp
from jax import lax
from jax.experimental import pallas as pl
from jax.experimental.pallas import tpu as pltpu
from jax.sharding import PartitionSpec as P

HEADS = 16
KVH = 4
HD = 128
GROUP = HEADS // KVH
D = 2048
CH = 64
BLK = 128
KVW = KVH * HD
KEYS = BLK + CH
SCALE = HD ** (-0.5)
CHIPS = 8
ROWS = D // CHIPS
HALF = ROWS // 2
CHUNKS = 4
STEP = D // CHUNKS
F32 = jnp.float32
BF16 = jnp.bfloat16

VMEM = pltpu.VMEM
ANY = pl.ANY
SMEM = pltpu.SMEM


def nt(a, b):
    return lax.dot_general(a, b, (((1,), (1,)), ((), ())), preferred_element_type=F32)


def nn(a, b):
    return lax.dot_general(a, b, (((1,), (0,)), ((), ())), preferred_element_type=F32)


def tn(a, b):
    return lax.dot_general(a, b, (((0,), (0,)), ((), ())), preferred_element_type=F32)


def stacked(ref, g):
    return jnp.concatenate(
        [ref[:, (g * GROUP + j) * HD : (g * GROUP + j + 1) * HD] for j in range(GROUP)], axis=0
    )


def softmax_t(score):
    score = score * SCALE
    key_at = lax.broadcasted_iota(jnp.int32, (CH, GROUP * CH), 0)
    row_at = lax.broadcasted_iota(jnp.int32, (CH, GROUP * CH), 1) % CH
    own = jnp.where(key_at <= row_at, score[BLK:], -jnp.inf)
    score = jnp.concatenate([score[:BLK], own], axis=0)
    raised = jnp.exp(score - jnp.max(score, axis=0, keepdims=True))
    return raised * (1.0 / jnp.sum(raised, axis=0, keepdims=True))


def section_kernel(
    ids_h, hidb_h, hidf_h, qb_h, qf_h, g_h, pk_h, pv_h, wk_h, wv_h,
    send_h, fwd_h, back_h, pkg_h, pvg_h, gs_h, keys_h,
    ids, hid, qb, qf, g, keys, values, weight, own, fwd, back, pkg, pvg, gs, sem, wsem, osem,
):
    rows = (pl.ds(0, CH), pl.ds(CH, CH))
    prefix = pl.ds(0, BLK)
    named = pltpu.make_async_copy(ids_h, ids, sem.at[9])
    named.start()
    load = [
        pltpu.make_async_copy(hidb_h, hid.at[rows[0]], sem.at[0]),
        pltpu.make_async_copy(hidf_h, hid.at[rows[1]], sem.at[1]),
        pltpu.make_async_copy(qb_h, qb, sem.at[2]),
        pltpu.make_async_copy(g_h, g, sem.at[3]),
        pltpu.make_async_copy(qf_h, qf, sem.at[4]),
    ]
    wload = []
    for h in range(KVH):
        at = pl.ds(h * HD, HD)
        for i, src in enumerate((wk_h, wv_h)):
            to = weight.at[:, pl.ds((2 * h + i) * HD, HD)]
            wload.append(pltpu.make_async_copy(src.at[:, at], to, wsem.at[2 * h + i]))
    for copy in load[:2] + wload + load[2:]:
        copy.start()
    named.wait()
    for group, block in ((0, ids[1]), (1, ids[0])):
        for i, (src, dst) in enumerate(((pk_h, keys), (pv_h, values))):
            to = dst.at[group, prefix]
            copy = pltpu.make_async_copy(src.at[block], to, sem.at[5 + 2 * group + i])
            copy.start()
            load.append(copy)
    out = []

    def put(src, dst):
        copy = pltpu.make_async_copy(src, dst, osem.at[len(out)])
        copy.start()
        out.append(copy)

    load[0].wait()
    for t in range(CHIPS):
        put(hid.at[rows[0], pl.ds(t * ROWS, ROWS)], send_h.at[t, :, pl.ds(0, ROWS)])
    load[1].wait()

    def columns(h):
        return slice(h * HD, (h + 1) * HD)

    def project(h):
        wload[2 * h].wait()
        wload[2 * h + 1].wait()
        new = nn(hid[...], weight[:, 2 * h * HD : 2 * (h + 1) * HD]).astype(BF16)
        for group in range(2):
            keys[group, BLK:, columns(h)] = new[group * CH : (group + 1) * CH, :HD]
            values[group, BLK:, columns(h)] = new[group * CH : (group + 1) * CH, HD:]

    def backward(heads):
        query = {h: stacked(qb, h) for h in heads}
        grad = {h: stacked(g, h) for h in heads}
        score = {h: nt(keys[0, :, columns(h)], query[h]) for h in heads}
        grad_probs = {h: nt(values[0, :, columns(h)], grad[h]) for h in heads}
        for h in heads:
            probs = softmax_t(score[h])
            inner = jnp.sum(probs * grad_probs[h], axis=0, keepdims=True)
            grad_scores = (probs * (grad_probs[h] - inner) * SCALE).astype(BF16)
            gs[h] = grad_scores
            key_grads = nn(grad_scores, query[h])
            value_grads = nn(probs.astype(BF16), grad[h])
            own[:, 2 * h * HD : (2 * h + 1) * HD] = key_grads[BLK:].astype(BF16)
            own[:, (2 * h + 1) * HD : 2 * (h + 1) * HD] = value_grads[BLK:].astype(BF16)
            pkg[:, columns(h)] = key_grads[:BLK].astype(BF16)
            pvg[:, columns(h)] = value_grads[:BLK].astype(BF16)

    def forward(heads):
        score = {h: nt(keys[1, :, columns(h)], stacked(qf, h)) for h in heads}
        for h in heads:
            attended = tn(softmax_t(score[h]).astype(BF16), values[1, :, columns(h)])
            for j in range(GROUP):
                at = columns(h * GROUP + j)
                fwd[:, at] = (
                    hid[CH:, at].astype(F32) + attended[j * CH : (j + 1) * CH]
                ).astype(BF16)

    def backed():
        for c in range(CHUNKS):
            at = slice(c * STEP, (c + 1) * STEP)
            back[:, at] = (g[:, at].astype(F32) + nt(own[...], weight[at, :])).astype(BF16)

    def sent():
        for t in range(CHIPS):
            put(own, send_h.at[t, :, pl.ds(ROWS, 2 * KVW)])
        put(pkg, pkg_h)
        put(pvg, pvg_h)
        put(gs, gs_h)
        put(keys.at[0], keys_h)

    for h in range(KVH):
        project(h)
    for copy in load[2:]:
        copy.wait()
    backward(range(KVH))
    sent()
    forward(range(KVH))
    backed()
    put(back, back_h)
    put(fwd, fwd_h)
    for copy in out:
        copy.wait()


def query_kernel(gs, keys, out):
    for h in range(KVH):
        grad = tn(gs[h], keys[:, h * HD : (h + 1) * HD])
        for j in range(GROUP):
            cols = slice((h * GROUP + j) * HD, (h * GROUP + j + 1) * HD)
            out[:, cols] = grad[j * CH : (j + 1) * CH].astype(BF16)


def weight_kernel(core, recv, mine, theirs):
    here = core[0]
    grads = recv[:, :, ROWS:].reshape(CHIPS * CH, 2 * KVW)
    low = tn(recv[:, :, :HALF].reshape(CHIPS * CH, HALF), grads)
    high = tn(recv[:, :, HALF:ROWS].reshape(CHIPS * CH, HALF), grads)
    first = here == 0
    mine[...] = jnp.where(first, low, high)
    theirs[...] = jnp.where(first, high, low).astype(BF16)


def sum_kernel(core, mine, both, fwd_in, back_in, key_grad, value_grad, fwd_out, back_out, sem):
    moves = [
        pltpu.make_async_copy(fwd_in, fwd_out, sem.at[0]),
        pltpu.make_async_copy(back_in, back_out, sem.at[1]),
    ]
    for copy in moves:
        copy.start()
    total = mine[...] + both[1 - core[0]].astype(F32)
    for h in range(KVH):
        at = slice(h * HD, (h + 1) * HD)
        key_grad[:, at] = total[:, 2 * h * HD : (2 * h + 1) * HD].astype(BF16)
        value_grad[:, at] = total[:, (2 * h + 1) * HD : 2 * (h + 1) * HD].astype(BF16)
    for copy in moves:
        copy.wait()


def call(kernel, outs, scratch, flops, in_specs, out_specs, size=62):
    return pl.pallas_call(
        kernel,
        out_shape=[jax.ShapeDtypeStruct(s, t) for s, t in outs],
        in_specs=in_specs,
        out_specs=out_specs,
        scratch_shapes=scratch,
        compiler_params=pltpu.CompilerParams(vmem_limit_bytes=size * 1024 * 1024),
        cost_estimate=pl.CostEstimate(flops=flops, bytes_accessed=6 << 20, transcendentals=200000),
    )


def spec(space):
    return pl.BlockSpec(memory_space=space)


def section_call(*arrays):
    dma = pltpu.SemaphoreType.DMA
    wide, kv = (CH, D), (KEYS, KVW)
    return call(
        section_kernel,
        [
            ((CHIPS, CH, ROWS + 2 * KVW), BF16),
            (wide, BF16),
            (wide, BF16),
            ((BLK, KVW), BF16),
            ((BLK, KVW), BF16),
            ((KVH, KEYS, GROUP * CH), BF16),
            (kv, BF16),
        ],
        [SMEM((2,), jnp.int32), VMEM((2 * CH, D), BF16)]
        + [VMEM(wide, BF16)] * 3
        + [VMEM((2,) + kv, BF16)] * 2
        + [VMEM((D, 2 * KVW), BF16), VMEM((CH, 2 * KVW), BF16)]
        + [VMEM(wide, BF16)] * 2
        + [VMEM((BLK, KVW), BF16)] * 2
        + [VMEM((KVH, KEYS, GROUP * CH), BF16), dma((10,)), dma((2 * KVH,)), dma((22,))],
        1_600_000_000,
        [spec(ANY)] * 10,
        [spec(ANY)] * 7,
    )(*arrays)


def along(value, axis, steps, wrap):
    count = lax.axis_size(axis)
    pairs = [(i, (i + steps) % count) for i in range(count) if wrap or 0 <= i + steps < count]
    return lax.ppermute(value, axis, pairs)


def per_device(
    fwd_hidden, fwd_query, bwd_hidden, bwd_query, bwd_grad,
    prefix_keys, prefix_values, key_weight, value_weight, block_ids,
):
    count = lax.axis_size("dp")
    dma = pltpu.SemaphoreType.DMA
    wide = (CH, D)
    ids = block_ids.reshape(2)
    send, out_fwd, out_bwd, pkg, pvg, gs, keys_bwd = section_call(
        ids, bwd_hidden[0, 0], fwd_hidden[0, 0], bwd_query[0, 0], fwd_query[0, 0], bwd_grad[0, 0],
        prefix_keys[0, 0], prefix_values[0, 0], key_weight[0], value_weight[0],
    )
    same_core = [[2 * t + c for t in range(count // 2)] for c in range(2)]
    pairs = [[2 * t, 2 * t + 1] for t in range(count // 2)]
    recv = lax.all_to_all(send, "dp", 0, 0, tiled=True, axis_index_groups=same_core)
    next_hidden = along(out_fwd, "section", 1, True)
    prev_grad = along(out_bwd, "section", -1, False)
    (query_grad,) = call(
        query_kernel,
        [(wide, BF16)],
        [],
        100_000_000,
        [spec(VMEM)] * 2,
        [spec(VMEM)],
        16,
    )(gs, keys_bwd)
    core = lax.axis_index("dp") & 1
    mine, theirs = call(
        weight_kernel,
        [((HALF, 2 * KVW), F32), ((HALF, 2 * KVW), BF16)],
        [],
        270_000_000,
        [spec(SMEM), spec(VMEM)],
        [spec(VMEM)] * 2,
        16,
    )(core.reshape(1), recv)
    both = lax.all_gather(theirs, "dp", axis=0, axis_index_groups=pairs)
    key_weight_grad, value_weight_grad, next_hidden, prev_grad = call(
        sum_kernel,
        [((HALF, KVW), BF16)] * 2 + [(wide, BF16)] * 2,
        [dma((2,))],
        1_000_000,
        [spec(SMEM)] + [spec(VMEM)] * 2 + [spec(ANY)] * 2,
        [spec(VMEM)] * 2 + [spec(ANY)] * 2,
        16,
    )(core.reshape(1), mine, both, next_hidden, prev_grad)
    return (
        next_hidden[None, None],
        prev_grad[None, None],
        query_grad[None, None],
        pkg[None, None, None],
        pvg[None, None, None],
        key_weight_grad[None],
        value_weight_grad[None],
    )


def solution(mesh):
    device = P("section", "dp")
    return jax.shard_map(
        per_device,
        mesh=mesh,
        in_specs=(device,) * 7 + (P("section"),) * 2 + (device,),
        out_specs=(device,) * 5 + (P("section", "dp"),) * 2,
        check_vma=False,
    )
```

time: 53.4 us -> 45.8 us (0.86)
  waiting for transfers between devices: 19.8 us -> 5.04 us
  blocking collectives: 4.59 us -> 17.9 us
  Pallas kernels: 15 us -> 10 us
  local copies, waits for them, and re-layouts: 1.41 us -> 0.02 us
    ppermute x2, waiting for transfers between devices: 19.8 us -> 0.01 us  [along(): return lax.ppermute(value, axis, pairs)]
    all_gather x1, blocking collectives: 4.59 us -> 17.9 us  [per_device(): both = lax.all_gather(theirs, 'dp', axis=0, axis_index_groups=pairs)]
    all_to_all x1, waiting for transfers between devices: 0.01 us -> 5.04 us  [per_device(): lax.all_to_all(send, 'dp', 0, 0, tiled=True, axis_index_groups=same_core)]
    pallas_call x3 -> x2, Pallas kernels: 13.5 us -> 8.52 us  [the longest x1 7.01 us: section_call(): call(section_kernel, [((CHIPS, CH, ROWS + 2 * KVW), BF16), (wide, BF16),...]
    unnamed x6 -> x8, local copies, waits for them, and re-layouts: 1.41 us -> 0.02 us
  transfers between devices with their start and end apart: 3 -> 3, of which waited for: 1 -> 1; matrix products, arithmetic and copies ran while one was open for 0% -> 0% of each run, Pallas kernels for 14% -> 3%
where the time goes in v2:
time: 45.8 us; the launch traced here: 45.5 us
  blocking collectives  17.9 us (39%)
  starting transfers between devices  11.7 us (26%)
  Pallas kernels  10 us (22%)
  waiting for transfers between devices  5.04 us (11%)
  between operations  0.73 us (2%)
    all_gather x1, blocking collectives, per_device(): both = lax.all_gather(theirs, 'dp', axis=0, axis_index_groups=pairs)  17.9 us
    pallas_call x1, Pallas kernels, section_call(): call(section_kernel, [((CHIPS, CH, ROWS + 2 * KVW), BF16), (wide, BF16),...  7.01 us
    all_to_all x1, starting transfers between devices, per_device(): lax.all_to_all(send, 'dp', 0, 0, tiled=True, axis_index_groups=same_core)  6.09 us
    ppermute x2, starting transfers between devices, along(): return lax.ppermute(value, axis, pairs)  5.65 us
    all_to_all x1, waiting for transfers between devices, per_device(): lax.all_to_all(send, 'dp', 0, 0, tiled=True, axis_index_groups=same_core)  5.04 us
    pallas_call x1, Pallas kernels, per_device(): call(sum_kernel, [((HALF, KVW), BF16)] * 2 + [(wide, BF16)] * 2, [dma((2,...  1.5 us
    pallas_call x1, Pallas kernels, per_device(): call(query_kernel, [(wide, BF16)], [], 100000000, [spec(VMEM)] * 2, [spec...  1.06 us
  transfers between devices with their start and end apart: 3, of which 1 were waited for; matrix products, arithmetic and copies ran while one was open for 0% of the time, Pallas kernels for 3%

profile of v2, /device:TPU:1, one launch (start us, length us, event | category | flops | bytes accessed | tf_op | source)
XLA Modules:
  0.0 45.5 jit_solution(4141092093716357310)
XLA Ops:
  0.6 7.0 %shard_map.153 = (bf16[8,64,1280]{2,1,0:T(8,128)(2,1)}, bf16[64,2048]{1,0:T(8,128)(2,1)}, bf16[64,2048]{1,0:T(8,128)(2,1)}, bf16[128,512]{1,0:T(8,128)(2,1)}, bf...) custom-call(s32[2]{0:T(128)} %bitcast.30, bf16[64,2048]{1,0:T(8,128)(2,1)} %bitcast.22, ...), custom_call_target="tpu_custom_call" | custom-call | flops 1600000000 | bytes 6291456 | tf_op jit(solution)/shard_map/pallas_call | solution.py:222
  7.7 0.0 copy-start.3
  7.7 0.0 copy-start.2
  7.7 0.0 copy-start
  7.7 0.0 copy-start.1
  7.7 6.1 %all-to-all-start = ((bf16[8,64,1280]{2,1,0:T(8,128)(2,1)}), bf16[8,64,1280]{2,1,0:T(8,128)(2,1)S(1)}, u32[]{:S(2)}, u32[]{:S(2)}) async-start(bf16[8,64,1280]{2,1,0:T(8,128)(2,1)} %get-tuple-element.20), calls=%async_computation | async-start | bytes 2621440 | tf_op jit(solution)/shard_map/all_to_all | solution.py:266
  13.8 0.0 copy-done.3
  13.8 4.4 %collective-permute-start = (bf16[64,2048]{1,0:T(8,128)(2,1)S(1)}, bf16[64,2048]{1,0:T(8,128)(2,1)S(1)}, u32[]{:S(2)}, u32[]{:S(2)}) collective-permute-start(bf16[64,2048]{1,0:T(8,128)(2,1)S(1)} %copy-done.3), channel_id=1, source_target_pairs={{0,16},{16,32},{32,48},{48,64},{64,80},{80,96},{96,112},{112,128},... | collective-permute-start | bytes 786440 | tf_op jit(solution)/shard_map/ppermute | solution.py:249
  18.2 0.0 copy-done.2
  18.2 1.3 %collective-permute-start.1 = (bf16[64,2048]{1,0:T(8,128)(2,1)S(1)}, bf16[64,2048]{1,0:T(8,128)(2,1)S(1)}, u32[]{:S(2)}, u32[]{:S(2)}) collective-permute-start(bf16[64,2048]{1,0:T(8,128)(2,1)S(1)} %copy-done.2), channel_id=1, source_target_pairs={{16,0},{32,16},{48,32},{64,48},{80,64},{96,80},{112,96},{128,112},... | collective-permute-start | bytes 786440 | tf_op jit(solution)/shard_map/ppermute | solution.py:249
  19.5 0.0 copy-done
  19.5 0.0 copy-done.1
  19.5 1.1 %shard_map.156 = bf16[64,2048]{1,0:T(8,128)(2,1)} custom-call(bf16[4,192,256]{2,1,0:T(8,128)(2,1)S(1)} %copy-done, bf16[192,512]{1,0:T(8,128)(2,1)S(1)} %copy-done.1), custom_call_target="tpu_custom_call" | custom-call | flops 100000000 | bytes 6291456 | tf_op jit(solution)/shard_map/pallas_call | solution.py:269
  20.6 5.0 %all-to-all-done.recv = bf16[8,64,1280]{2,1,0:T(8,128)(2,1)S(1)} async-done(((bf16[8,64,1280]{2,1,0:T(8,128)(2,1)}), bf16[8,64,1280]{2,1,0:T(8,128)(2,1)S(1)}, u32[]{:S(2)}, u32[]{:S(2)}) %all-to-all-start) | async-done | bytes 1310752 | tf_op jit(solution)/shard_map/all_to_all | solution.py:266
  25.6 0.5 %shard_map.154 = (f32[128,1024]{1,0:T(8,128)S(1)}, bf16[128,1024]{1,0:T(8,128)(2,1)S(1)}) custom-call(s32[1]{0:T(128)} %bitcast.core, bf16[8,64,1280]{2,1,0:T(8,128)(2,1)S(1)} %all-to-all-done.recv), custom_call_target="tpu_custom_call" | custom-call | flops 270000000 | bytes 6291456 | tf_op jit(solution)/shard_map/pallas_call | solution.py:279
  26.1 17.9 %all-gather = bf16[256,1024]{1,0:T(8,128)(2,1)S(1)} all-gather(bf16[128,1024]{1,0:T(8,128)(2,1)S(1)} %get-tuple-element.22), channel_id=2, replica_groups={{0,1},{2,3},{4,5},{6,7},{8,9},{10,11},{12,13},{14,15},{16,17},{18,19},{..., dimensions={0}, use_global_device_ids=true | all-gather | bytes 786432 | tf_op jit(solution)/shard_map/all_gather | solution.py:288
  44.0 0.0 collective-permute-done.fwd_in
  44.0 0.0 collective-permute-done.1.back_in
  44.0 1.5 %shard_map.155 = (bf16[128,512]{1,0:T(8,128)(2,1)}, bf16[128,512]{1,0:T(8,128)(2,1)}, bf16[64,2048]{1,0:T(8,128)(2,1)}, bf16[64,2048]{1,0:T(8,128)(2,1)}) custom-call(s32[1]{0:T(128)} %bitcast.core, f32[128,1024]{1,0:T(8,128)S(1)} %get-tuple-element.21.mine, bf16[2,128,1024]{2,1,0:T(8,128)(2,1)S(1)} %bitcast.19, ...), custom_call_target="tpu_custom_call" | custom-call | flops 1000000 | bytes 6291456 | tf_op jit(solution)/shard_map/pallas_call | solution.py:289
Async XLA Ops:
  7.7 6.1 %copy-start.3 = (bf16[64,2048]{1,0:T(8,128)(2,1)S(1)}, bf16[64,2048]{1,0:T(8,128)(2,1)}, u32[]{:S(2)}) copy-start(bf16[64,2048]{1,0:T(8,128)(2,1)} %get-tuple-element.23) | copy-start | bytes 786436
  7.7 10.5 %copy-start.2 = (bf16[64,2048]{1,0:T(8,128)(2,1)S(1)}, bf16[64,2048]{1,0:T(8,128)(2,1)}, u32[]{:S(2)}) copy-start(bf16[64,2048]{1,0:T(8,128)(2,1)} %get-tuple-element.24) | copy-start | bytes 786436
  7.7 11.8 %copy-start = (bf16[4,192,256]{2,1,0:T(8,128)(2,1)S(1)}, bf16[4,192,256]{2,1,0:T(8,128)(2,1)}, u32[]{:S(2)}) copy-start(bf16[4,192,256]{2,1,0:T(8,128)(2,1)} %get-tuple-element.27.gs) | copy-start | bytes 1179652
  7.7 11.8 %copy-start.1 = (bf16[192,512]{1,0:T(8,128)(2,1)S(1)}, bf16[192,512]{1,0:T(8,128)(2,1)}, u32[]{:S(2)}) copy-start(bf16[192,512]{1,0:T(8,128)(2,1)} %get-tuple-element.28.keys) | copy-start | bytes 589828
  7.7 17.9 %all-to-all-start = ((bf16[8,64,1280]{2,1,0:T(8,128)(2,1)}), bf16[8,64,1280]{2,1,0:T(8,128)(2,1)S(1)}, u32[]{:S(2)}, u32[]{:S(2)}) async-start(bf16[8,64,1280]{2,1,0:T(8,128)(2,1)} %get-tuple-element.20), calls=%async_computation | async-start | bytes 2621440 | tf_op jit(solution)/shard_map/all_to_all | solution.py:266
  13.8 30.2 %collective-permute-start = (bf16[64,2048]{1,0:T(8,128)(2,1)S(1)}, bf16[64,2048]{1,0:T(8,128)(2,1)S(1)}, u32[]{:S(2)}, u32[]{:S(2)}) collective-permute-start(bf16[64,2048]{1,0:T(8,128)(2,1)S(1)} %copy-done.3), channel_id=1, source_target_pairs={{0,16},{16,32},{32,48},{48,64},{64,80},{80,96},{96,112},{112,128},... | collective-permute-start | bytes 786440 | tf_op jit(solution)/shard_map/ppermute | solution.py:249
  18.2 25.9 %collective-permute-start.1 = (bf16[64,2048]{1,0:T(8,128)(2,1)S(1)}, bf16[64,2048]{1,0:T(8,128)(2,1)S(1)}, u32[]{:S(2)}, u32[]{:S(2)}) collective-permute-start(bf16[64,2048]{1,0:T(8,128)(2,1)S(1)} %copy-done.2), channel_id=1, source_target_pairs={{16,0},{32,16},{48,32},{64,48},{80,64},{96,80},{112,96},{128,112},... | collective-permute-start | bytes 786440 | tf_op jit(solution)/shard_map/ppermute | solution.py:249

commit v3 on v2

--- a/solution.py
+++ b/solution.py
@@ -184,18 +184,26 @@
     theirs[...] = jnp.where(first, high, low).astype(BF16)
 
 
-def sum_kernel(core, mine, both, fwd_in, back_in, key_grad, value_grad, fwd_out, back_out, sem):
+def sum_kernel(
+    core, mine, both, fwd_in, back_in,
+    key_out, value_out, fwd_out, back_out,
+    key_grad, value_grad, sem,
+):
     moves = [
         pltpu.make_async_copy(fwd_in, fwd_out, sem.at[0]),
         pltpu.make_async_copy(back_in, back_out, sem.at[1]),
+        pltpu.make_async_copy(key_grad, key_out, sem.at[2]),
+        pltpu.make_async_copy(value_grad, value_out, sem.at[3]),
     ]
-    for copy in moves:
+    for copy in moves[:2]:
         copy.start()
     total = mine[...] + both[1 - core[0]].astype(F32)
     for h in range(KVH):
         at = slice(h * HD, (h + 1) * HD)
         key_grad[:, at] = total[:, 2 * h * HD : (2 * h + 1) * HD].astype(BF16)
         value_grad[:, at] = total[:, (2 * h + 1) * HD : 2 * (h + 1) * HD].astype(BF16)
+    for copy in moves[2:]:
+        copy.start()
     for copy in moves:
         copy.wait()
 
@@ -289,10 +297,10 @@
     key_weight_grad, value_weight_grad, next_hidden, prev_grad = call(
         sum_kernel,
         [((HALF, KVW), BF16)] * 2 + [(wide, BF16)] * 2,
-        [dma((2,))],
+        [VMEM((HALF, KVW), BF16)] * 2 + [dma((4,))],
         1_000_000,
         [spec(SMEM)] + [spec(VMEM)] * 2 + [spec(ANY)] * 2,
-        [spec(VMEM)] * 2 + [spec(ANY)] * 2,
+        [spec(ANY)] * 4,
         16,
     )(core.reshape(1), mine, both, next_hidden, prev_grad)
     return (

time: 45.8 us -> 45.2 us (0.987)
  Pallas kernels: 10 us -> 9.45 us
    pallas_call x1, Pallas kernels: 1.5 us -> 0.91 us  [per_device(): call(sum_kernel, [((HALF, KVW), BF16)] * 2 + [(wide, BF16)] * 2, [VMEM((H...]
where the time goes in v3:
time: 45.2 us; the launch traced here: 44.9 us
  blocking collectives  17.9 us (40%)
  starting transfers between devices  11.7 us (26%)
  Pallas kernels  9.45 us (21%)
  waiting for transfers between devices  5.04 us (11%)
  between operations  0.73 us (2%)
    all_gather x1, blocking collectives, per_device(): both = lax.all_gather(theirs, 'dp', axis=0, axis_index_groups=pairs)  17.9 us
    pallas_call x1, Pallas kernels, section_call(): call(section_kernel, [((CHIPS, CH, ROWS + 2 * KVW), BF16), (wide, BF16),...  7.01 us
    all_to_all x1, starting transfers between devices, per_device(): lax.all_to_all(send, 'dp', 0, 0, tiled=True, axis_index_groups=same_core)  6.09 us
    ppermute x2, starting transfers between devices, along(): return lax.ppermute(value, axis, pairs)  5.65 us
    all_to_all x1, waiting for transfers between devices, per_device(): lax.all_to_all(send, 'dp', 0, 0, tiled=True, axis_index_groups=same_core)  5.04 us
    pallas_call x1, Pallas kernels, per_device(): call(query_kernel, [(wide, BF16)], [], 100000000, [spec(VMEM)] * 2, [spec...  1.06 us
    pallas_call x1, Pallas kernels, per_device(): call(sum_kernel, [((HALF, KVW), BF16)] * 2 + [(wide, BF16)] * 2, [VMEM((H...  0.91 us
  transfers between devices with their start and end apart: 3, of which 1 were waited for; matrix products, arithmetic and copies ran while one was open for 0% of the time, Pallas kernels for 3%

profile of v3, /device:TPU:1, one launch (start us, length us, event | category | flops | bytes accessed | tf_op | source)
XLA Modules:
  0.0 44.9 jit_solution(8684162410305095523)
XLA Ops:
  0.6 7.0 %shard_map.153 = (bf16[8,64,1280]{2,1,0:T(8,128)(2,1)}, bf16[64,2048]{1,0:T(8,128)(2,1)}, bf16[64,2048]{1,0:T(8,128)(2,1)}, bf16[128,512]{1,0:T(8,128)(2,1)}, bf...) custom-call(s32[2]{0:T(128)} %bitcast.30, bf16[64,2048]{1,0:T(8,128)(2,1)} %bitcast.22, ...), custom_call_target="tpu_custom_call" | custom-call | flops 1600000000 | bytes 6291456 | tf_op jit(solution)/shard_map/pallas_call | solution.py:230
  7.7 0.0 copy-start.3
  7.7 0.0 copy-start.2
  7.7 0.0 copy-start
  7.7 0.0 copy-start.1
  7.7 6.1 %all-to-all-start = ((bf16[8,64,1280]{2,1,0:T(8,128)(2,1)}), bf16[8,64,1280]{2,1,0:T(8,128)(2,1)S(1)}, u32[]{:S(2)}, u32[]{:S(2)}) async-start(bf16[8,64,1280]{2,1,0:T(8,128)(2,1)} %get-tuple-element.20), calls=%async_computation | async-start | bytes 2621440 | tf_op jit(solution)/shard_map/all_to_all | solution.py:274
  13.8 0.0 copy-done.3
  13.8 4.4 %collective-permute-start = (bf16[64,2048]{1,0:T(8,128)(2,1)S(1)}, bf16[64,2048]{1,0:T(8,128)(2,1)S(1)}, u32[]{:S(2)}, u32[]{:S(2)}) collective-permute-start(bf16[64,2048]{1,0:T(8,128)(2,1)S(1)} %copy-done.3), channel_id=1, source_target_pairs={{0,16},{16,32},{32,48},{48,64},{64,80},{80,96},{96,112},{112,128},... | collective-permute-start | bytes 786440 | tf_op jit(solution)/shard_map/ppermute | solution.py:257
  18.2 0.0 copy-done.2
  18.2 1.3 %collective-permute-start.1 = (bf16[64,2048]{1,0:T(8,128)(2,1)S(1)}, bf16[64,2048]{1,0:T(8,128)(2,1)S(1)}, u32[]{:S(2)}, u32[]{:S(2)}) collective-permute-start(bf16[64,2048]{1,0:T(8,128)(2,1)S(1)} %copy-done.2), channel_id=1, source_target_pairs={{16,0},{32,16},{48,32},{64,48},{80,64},{96,80},{112,96},{128,112},... | collective-permute-start | bytes 786440 | tf_op jit(solution)/shard_map/ppermute | solution.py:257
  19.5 0.0 copy-done
  19.5 0.0 copy-done.1
  19.5 1.1 %shard_map.156 = bf16[64,2048]{1,0:T(8,128)(2,1)} custom-call(bf16[4,192,256]{2,1,0:T(8,128)(2,1)S(1)} %copy-done, bf16[192,512]{1,0:T(8,128)(2,1)S(1)} %copy-done.1), custom_call_target="tpu_custom_call" | custom-call | flops 100000000 | bytes 6291456 | tf_op jit(solution)/shard_map/pallas_call | solution.py:277
  20.6 5.0 %all-to-all-done.recv = bf16[8,64,1280]{2,1,0:T(8,128)(2,1)S(1)} async-done(((bf16[8,64,1280]{2,1,0:T(8,128)(2,1)}), bf16[8,64,1280]{2,1,0:T(8,128)(2,1)S(1)}, u32[]{:S(2)}, u32[]{:S(2)}) %all-to-all-start) | async-done | bytes 1310752 | tf_op jit(solution)/shard_map/all_to_all | solution.py:274
  25.6 0.5 %shard_map.154 = (f32[128,1024]{1,0:T(8,128)S(1)}, bf16[128,1024]{1,0:T(8,128)(2,1)S(1)}) custom-call(s32[1]{0:T(128)} %bitcast.core, bf16[8,64,1280]{2,1,0:T(8,128)(2,1)S(1)} %all-to-all-done.recv), custom_call_target="tpu_custom_call" | custom-call | flops 270000000 | bytes 6291456 | tf_op jit(solution)/shard_map/pallas_call | solution.py:287
  26.1 17.9 %all-gather = bf16[256,1024]{1,0:T(8,128)(2,1)S(1)} all-gather(bf16[128,1024]{1,0:T(8,128)(2,1)S(1)} %get-tuple-element.22), channel_id=2, replica_groups={{0,1},{2,3},{4,5},{6,7},{8,9},{10,11},{12,13},{14,15},{16,17},{18,19},{..., dimensions={0}, use_global_device_ids=true | all-gather | bytes 786432 | tf_op jit(solution)/shard_map/all_gather | solution.py:296
  44.0 0.0 collective-permute-done.fwd_in
  44.0 0.0 collective-permute-done.1.back_in
  44.0 0.9 %shard_map.155 = (bf16[128,512]{1,0:T(8,128)(2,1)}, bf16[128,512]{1,0:T(8,128)(2,1)}, bf16[64,2048]{1,0:T(8,128)(2,1)}, bf16[64,2048]{1,0:T(8,128)(2,1)}) custom-call(s32[1]{0:T(128)} %bitcast.core, f32[128,1024]{1,0:T(8,128)S(1)} %get-tuple-element.21.mine, bf16[2,128,1024]{2,1,0:T(8,128)(2,1)S(1)} %bitcast.19, ...), custom_call_target="tpu_custom_call" | custom-call | flops 1000000 | bytes 6291456 | tf_op jit(solution)/shard_map/pallas_call | solution.py:297
Async XLA Ops:
  7.7 6.1 %copy-start.3 = (bf16[64,2048]{1,0:T(8,128)(2,1)S(1)}, bf16[64,2048]{1,0:T(8,128)(2,1)}, u32[]{:S(2)}) copy-start(bf16[64,2048]{1,0:T(8,128)(2,1)} %get-tuple-element.23) | copy-start | bytes 786436
  7.7 10.5 %copy-start.2 = (bf16[64,2048]{1,0:T(8,128)(2,1)S(1)}, bf16[64,2048]{1,0:T(8,128)(2,1)}, u32[]{:S(2)}) copy-start(bf16[64,2048]{1,0:T(8,128)(2,1)} %get-tuple-element.24) | copy-start | bytes 786436
  7.7 11.8 %copy-start = (bf16[4,192,256]{2,1,0:T(8,128)(2,1)S(1)}, bf16[4,192,256]{2,1,0:T(8,128)(2,1)}, u32[]{:S(2)}) copy-start(bf16[4,192,256]{2,1,0:T(8,128)(2,1)} %get-tuple-element.27.gs) | copy-start | bytes 1179652
  7.7 11.8 %copy-start.1 = (bf16[192,512]{1,0:T(8,128)(2,1)S(1)}, bf16[192,512]{1,0:T(8,128)(2,1)}, u32[]{:S(2)}) copy-start(bf16[192,512]{1,0:T(8,128)(2,1)} %get-tuple-element.28.keys) | copy-start | bytes 589828
  7.7 17.9 %all-to-all-start = ((bf16[8,64,1280]{2,1,0:T(8,128)(2,1)}), bf16[8,64,1280]{2,1,0:T(8,128)(2,1)S(1)}, u32[]{:S(2)}, u32[]{:S(2)}) async-start(bf16[8,64,1280]{2,1,0:T(8,128)(2,1)} %get-tuple-element.20), calls=%async_computation | async-start | bytes 2621440 | tf_op jit(solution)/shard_map/all_to_all | solution.py:274
  13.8 30.2 %collective-permute-start = (bf16[64,2048]{1,0:T(8,128)(2,1)S(1)}, bf16[64,2048]{1,0:T(8,128)(2,1)S(1)}, u32[]{:S(2)}, u32[]{:S(2)}) collective-permute-start(bf16[64,2048]{1,0:T(8,128)(2,1)S(1)} %copy-done.3), channel_id=1, source_target_pairs={{0,16},{16,32},{32,48},{48,64},{64,80},{80,96},{96,112},{112,128},... | collective-permute-start | bytes 786440 | tf_op jit(solution)/shard_map/ppermute | solution.py:257
  18.2 25.9 %collective-permute-start.1 = (bf16[64,2048]{1,0:T(8,128)(2,1)S(1)}, bf16[64,2048]{1,0:T(8,128)(2,1)S(1)}, u32[]{:S(2)}, u32[]{:S(2)}) collective-permute-start(bf16[64,2048]{1,0:T(8,128)(2,1)S(1)} %copy-done.2), channel_id=1, source_target_pairs={{16,0},{32,16},{48,32},{64,48},{80,64},{96,80},{112,96},{128,112},... | collective-permute-start | bytes 786440 | tf_op jit(solution)/shard_map/ppermute | solution.py:257

commit v4 on v3

--- a/solution.py
+++ b/solution.py
@@ -75,11 +75,11 @@
         pltpu.make_async_copy(qf_h, qf, sem.at[4]),
     ]
     wload = []
-    for h in range(KVH):
-        at = pl.ds(h * HD, HD)
+    for c in range(CHUNKS):
+        at = pl.ds(c * STEP, STEP)
         for i, src in enumerate((wk_h, wv_h)):
-            to = weight.at[:, pl.ds((2 * h + i) * HD, HD)]
-            wload.append(pltpu.make_async_copy(src.at[:, at], to, wsem.at[2 * h + i]))
+            to = weight.at[at, pl.ds(i * KVW, KVW)]
+            wload.append(pltpu.make_async_copy(src.at[at], to, wsem.at[2 * c + i]))
     for copy in load[:2] + wload + load[2:]:
         copy.start()
     named.wait()
@@ -104,13 +104,18 @@
     def columns(h):
         return slice(h * HD, (h + 1) * HD)
 
-    def project(h):
-        wload[2 * h].wait()
-        wload[2 * h + 1].wait()
-        new = nn(hid[...], weight[:, 2 * h * HD : 2 * (h + 1) * HD]).astype(BF16)
+    def project():
+        total = None
+        for c in range(CHUNKS):
+            wload[2 * c].wait()
+            wload[2 * c + 1].wait()
+            at = slice(c * STEP, (c + 1) * STEP)
+            part = nn(hid[:, at], weight[at, :])
+            total = part if total is None else total + part
+        new = total.astype(BF16)
         for group in range(2):
-            keys[group, BLK:, columns(h)] = new[group * CH : (group + 1) * CH, :HD]
-            values[group, BLK:, columns(h)] = new[group * CH : (group + 1) * CH, HD:]
+            keys[group, BLK:, :] = new[group * CH : (group + 1) * CH, :KVW]
+            values[group, BLK:, :] = new[group * CH : (group + 1) * CH, KVW:]
 
     def backward(heads):
         query = {h: stacked(qb, h) for h in heads}
@@ -124,8 +129,8 @@
             gs[h] = grad_scores
             key_grads = nn(grad_scores, query[h])
             value_grads = nn(probs.astype(BF16), grad[h])
-            own[:, 2 * h * HD : (2 * h + 1) * HD] = key_grads[BLK:].astype(BF16)
-            own[:, (2 * h + 1) * HD : 2 * (h + 1) * HD] = value_grads[BLK:].astype(BF16)
+            own[:, columns(h)] = key_grads[BLK:].astype(BF16)
+            own[:, columns(KVH + h)] = value_grads[BLK:].astype(BF16)
             pkg[:, columns(h)] = key_grads[:BLK].astype(BF16)
             pvg[:, columns(h)] = value_grads[:BLK].astype(BF16)
 
@@ -152,8 +157,7 @@
         put(gs, gs_h)
         put(keys.at[0], keys_h)
 
-    for h in range(KVH):
-        project(h)
+    project()
     for copy in load[2:]:
         copy.wait()
     backward(range(KVH))
@@ -198,10 +202,8 @@
     for copy in moves[:2]:
         copy.start()
     total = mine[...] + both[1 - core[0]].astype(F32)
-    for h in range(KVH):
-        at = slice(h * HD, (h + 1) * HD)
-        key_grad[:, at] = total[:, 2 * h * HD : (2 * h + 1) * HD].astype(BF16)
-        value_grad[:, at] = total[:, (2 * h + 1) * HD : 2 * (h + 1) * HD].astype(BF16)
+    key_grad[...] = total[:, :KVW].astype(BF16)
+    value_grad[...] = total[:, KVW:].astype(BF16)
     for copy in moves[2:]:
         copy.start()
     for copy in moves:
@@ -244,7 +246,7 @@
         + [VMEM((D, 2 * KVW), BF16), VMEM((CH, 2 * KVW), BF16)]
         + [VMEM(wide, BF16)] * 2
         + [VMEM((BLK, KVW), BF16)] * 2
-        + [VMEM((KVH, KEYS, GROUP * CH), BF16), dma((10,)), dma((2 * KVH,)), dma((22,))],
+        + [VMEM((KVH, KEYS, GROUP * CH), BF16), dma((10,)), dma((2 * CHUNKS,)), dma((22,))],
         1_600_000_000,
         [spec(ANY)] * 10,
         [spec(ANY)] * 7,

time: 45.2 us -> 44.7 us (0.989)
  Pallas kernels: 9.45 us -> 8.94 us
    pallas_call x1, Pallas kernels: 7.01 us -> 6.51 us  [section_call(): call(section_kernel, [((CHIPS, CH, ROWS + 2 * KVW), BF16), (wide, BF16),...]
where the time goes in v4:
time: 44.7 us; the launch traced here: 44.4 us
  blocking collectives  17.9 us (40%)
  starting transfers between devices  11.7 us (26%)
  Pallas kernels  8.94 us (20%)
  waiting for transfers between devices  5.04 us (11%)
  between operations  0.73 us (2%)
    all_gather x1, blocking collectives, per_device(): both = lax.all_gather(theirs, 'dp', axis=0, axis_index_groups=pairs)  17.9 us
    pallas_call x1, Pallas kernels, section_call(): call(section_kernel, [((CHIPS, CH, ROWS + 2 * KVW), BF16), (wide, BF16),...  6.51 us
    all_to_all x1, starting transfers between devices, per_device(): lax.all_to_all(send, 'dp', 0, 0, tiled=True, axis_index_groups=same_core)  6.1 us
    ppermute x2, starting transfers between devices, along(): return lax.ppermute(value, axis, pairs)  5.65 us
    all_to_all x1, waiting for transfers between devices, per_device(): lax.all_to_all(send, 'dp', 0, 0, tiled=True, axis_index_groups=same_core)  5.04 us
    pallas_call x1, Pallas kernels, per_device(): call(query_kernel, [(wide, BF16)], [], 100000000, [spec(VMEM)] * 2, [spec...  1.06 us
    pallas_call x1, Pallas kernels, per_device(): call(sum_kernel, [((HALF, KVW), BF16)] * 2 + [(wide, BF16)] * 2, [VMEM((H...  0.91 us
  transfers between devices with their start and end apart: 3, of which 1 were waited for; matrix products, arithmetic and copies ran while one was open for 0% of the time, Pallas kernels for 3%

profile of v4, /device:TPU:1, one launch (start us, length us, event | category | flops | bytes accessed | tf_op | source)
XLA Modules:
  0.0 44.4 jit_solution(2574800288608937350)
XLA Ops:
  0.6 6.5 %shard_map.153 = (bf16[8,64,1280]{2,1,0:T(8,128)(2,1)}, bf16[64,2048]{1,0:T(8,128)(2,1)}, bf16[64,2048]{1,0:T(8,128)(2,1)}, bf16[128,512]{1,0:T(8,128)(2,1)}, bf...) custom-call(s32[2]{0:T(128)} %bitcast.30, bf16[64,2048]{1,0:T(8,128)(2,1)} %bitcast.22, ...), custom_call_target="tpu_custom_call" | custom-call | flops 1600000000 | bytes 6291456 | tf_op jit(solution)/shard_map/pallas_call | solution.py:232
  7.1 0.0 copy-start.3
  7.2 0.0 copy-start.2
  7.2 0.0 copy-start
  7.2 0.0 copy-start.1
  7.2 6.1 %all-to-all-start = ((bf16[8,64,1280]{2,1,0:T(8,128)(2,1)}), bf16[8,64,1280]{2,1,0:T(8,128)(2,1)S(1)}, u32[]{:S(2)}, u32[]{:S(2)}) async-start(bf16[8,64,1280]{2,1,0:T(8,128)(2,1)} %get-tuple-element.20), calls=%async_computation | async-start | bytes 2621440 | tf_op jit(solution)/shard_map/all_to_all | solution.py:276
  13.3 0.0 copy-done.3
  13.3 4.4 %collective-permute-start = (bf16[64,2048]{1,0:T(8,128)(2,1)S(1)}, bf16[64,2048]{1,0:T(8,128)(2,1)S(1)}, u32[]{:S(2)}, u32[]{:S(2)}) collective-permute-start(bf16[64,2048]{1,0:T(8,128)(2,1)S(1)} %copy-done.3), channel_id=1, source_target_pairs={{0,16},{16,32},{32,48},{48,64},{64,80},{80,96},{96,112},{112,128},... | collective-permute-start | bytes 786440 | tf_op jit(solution)/shard_map/ppermute | solution.py:259
  17.7 0.0 copy-done.2
  17.7 1.3 %collective-permute-start.1 = (bf16[64,2048]{1,0:T(8,128)(2,1)S(1)}, bf16[64,2048]{1,0:T(8,128)(2,1)S(1)}, u32[]{:S(2)}, u32[]{:S(2)}) collective-permute-start(bf16[64,2048]{1,0:T(8,128)(2,1)S(1)} %copy-done.2), channel_id=1, source_target_pairs={{16,0},{32,16},{48,32},{64,48},{80,64},{96,80},{112,96},{128,112},... | collective-permute-start | bytes 786440 | tf_op jit(solution)/shard_map/ppermute | solution.py:259
  19.0 0.0 copy-done
  19.0 0.0 copy-done.1
  19.0 1.1 %shard_map.156 = bf16[64,2048]{1,0:T(8,128)(2,1)} custom-call(bf16[4,192,256]{2,1,0:T(8,128)(2,1)S(1)} %copy-done, bf16[192,512]{1,0:T(8,128)(2,1)S(1)} %copy-done.1), custom_call_target="tpu_custom_call" | custom-call | flops 100000000 | bytes 6291456 | tf_op jit(solution)/shard_map/pallas_call | solution.py:279
  20.0 5.0 %all-to-all-done.recv = bf16[8,64,1280]{2,1,0:T(8,128)(2,1)S(1)} async-done(((bf16[8,64,1280]{2,1,0:T(8,128)(2,1)}), bf16[8,64,1280]{2,1,0:T(8,128)(2,1)S(1)}, u32[]{:S(2)}, u32[]{:S(2)}) %all-to-all-start) | async-done | bytes 1310752 | tf_op jit(solution)/shard_map/all_to_all | solution.py:276
  25.1 0.5 %shard_map.154 = (f32[128,1024]{1,0:T(8,128)S(1)}, bf16[128,1024]{1,0:T(8,128)(2,1)S(1)}) custom-call(s32[1]{0:T(128)} %bitcast.core, bf16[8,64,1280]{2,1,0:T(8,128)(2,1)S(1)} %all-to-all-done.recv), custom_call_target="tpu_custom_call" | custom-call | flops 270000000 | bytes 6291456 | tf_op jit(solution)/shard_map/pallas_call | solution.py:289
  25.6 17.9 %all-gather = bf16[256,1024]{1,0:T(8,128)(2,1)S(1)} all-gather(bf16[128,1024]{1,0:T(8,128)(2,1)S(1)} %get-tuple-element.22), channel_id=2, replica_groups={{0,1},{2,3},{4,5},{6,7},{8,9},{10,11},{12,13},{14,15},{16,17},{18,19},{..., dimensions={0}, use_global_device_ids=true | all-gather | bytes 786432 | tf_op jit(solution)/shard_map/all_gather | solution.py:298
  43.5 0.0 collective-permute-done.fwd_in
  43.5 0.0 collective-permute-done.1.back_in
  43.5 0.9 %shard_map.155 = (bf16[128,512]{1,0:T(8,128)(2,1)}, bf16[128,512]{1,0:T(8,128)(2,1)}, bf16[64,2048]{1,0:T(8,128)(2,1)}, bf16[64,2048]{1,0:T(8,128)(2,1)}) custom-call(s32[1]{0:T(128)} %bitcast.core, f32[128,1024]{1,0:T(8,128)S(1)} %get-tuple-element.21.mine, bf16[2,128,1024]{2,1,0:T(8,128)(2,1)S(1)} %bitcast.19, ...), custom_call_target="tpu_custom_call" | custom-call | flops 1000000 | bytes 6291456 | tf_op jit(solution)/shard_map/pallas_call | solution.py:299
Async XLA Ops:
  7.1 6.1 %copy-start.3 = (bf16[64,2048]{1,0:T(8,128)(2,1)S(1)}, bf16[64,2048]{1,0:T(8,128)(2,1)}, u32[]{:S(2)}) copy-start(bf16[64,2048]{1,0:T(8,128)(2,1)} %get-tuple-element.23) | copy-start | bytes 786436
  7.2 10.5 %copy-start.2 = (bf16[64,2048]{1,0:T(8,128)(2,1)S(1)}, bf16[64,2048]{1,0:T(8,128)(2,1)}, u32[]{:S(2)}) copy-start(bf16[64,2048]{1,0:T(8,128)(2,1)} %get-tuple-element.24) | copy-start | bytes 786436
  7.2 11.8 %copy-start = (bf16[4,192,256]{2,1,0:T(8,128)(2,1)S(1)}, bf16[4,192,256]{2,1,0:T(8,128)(2,1)}, u32[]{:S(2)}) copy-start(bf16[4,192,256]{2,1,0:T(8,128)(2,1)} %get-tuple-element.27.gs) | copy-start | bytes 1179652
  7.2 11.8 %copy-start.1 = (bf16[192,512]{1,0:T(8,128)(2,1)S(1)}, bf16[192,512]{1,0:T(8,128)(2,1)}, u32[]{:S(2)}) copy-start(bf16[192,512]{1,0:T(8,128)(2,1)} %get-tuple-element.28.keys) | copy-start | bytes 589828
  7.2 17.9 %all-to-all-start = ((bf16[8,64,1280]{2,1,0:T(8,128)(2,1)}), bf16[8,64,1280]{2,1,0:T(8,128)(2,1)S(1)}, u32[]{:S(2)}, u32[]{:S(2)}) async-start(bf16[8,64,1280]{2,1,0:T(8,128)(2,1)} %get-tuple-element.20), calls=%async_computation | async-start | bytes 2621440 | tf_op jit(solution)/shard_map/all_to_all | solution.py:276
  13.3 30.2 %collective-permute-start = (bf16[64,2048]{1,0:T(8,128)(2,1)S(1)}, bf16[64,2048]{1,0:T(8,128)(2,1)S(1)}, u32[]{:S(2)}, u32[]{:S(2)}) collective-permute-start(bf16[64,2048]{1,0:T(8,128)(2,1)S(1)} %copy-done.3), channel_id=1, source_target_pairs={{0,16},{16,32},{32,48},{48,64},{64,80},{80,96},{96,112},{112,128},... | collective-permute-start | bytes 786440 | tf_op jit(solution)/shard_map/ppermute | solution.py:259
  17.7 25.8 %collective-permute-start.1 = (bf16[64,2048]{1,0:T(8,128)(2,1)S(1)}, bf16[64,2048]{1,0:T(8,128)(2,1)S(1)}, u32[]{:S(2)}, u32[]{:S(2)}) collective-permute-start(bf16[64,2048]{1,0:T(8,128)(2,1)S(1)} %copy-done.2), channel_id=1, source_target_pairs={{16,0},{32,16},{48,32},{64,48},{80,64},{96,80},{112,96},{128,112},... | collective-permute-start | bytes 786440 | tf_op jit(solution)/shard_map/ppermute | solution.py:259

commit v5 on v4

--- a/solution.py
+++ b/solution.py
@@ -163,9 +163,9 @@
     backward(range(KVH))
     sent()
     forward(range(KVH))
+    put(fwd, fwd_h)
     backed()
     put(back, back_h)
-    put(fwd, fwd_h)
     for copy in out:
         copy.wait()
 
@@ -189,8 +189,8 @@
 
 
 def sum_kernel(
-    core, mine, both, fwd_in, back_in,
-    key_out, value_out, fwd_out, back_out,
+    core, mine, both, back_in, fwd_in,
+    key_out, value_out, back_out, fwd_out,
     key_grad, value_grad, sem,
 ):
     moves = [
@@ -274,8 +274,8 @@
     same_core = [[2 * t + c for t in range(count // 2)] for c in range(2)]
     pairs = [[2 * t, 2 * t + 1] for t in range(count // 2)]
     recv = lax.all_to_all(send, "dp", 0, 0, tiled=True, axis_index_groups=same_core)
+    prev_grad = along(out_bwd, "section", -1, False)
     next_hidden = along(out_fwd, "section", 1, True)
-    prev_grad = along(out_bwd, "section", -1, False)
     (query_grad,) = call(
         query_kernel,
         [(wide, BF16)],
@@ -296,7 +296,7 @@
         16,
     )(core.reshape(1), recv)
     both = lax.all_gather(theirs, "dp", axis=0, axis_index_groups=pairs)
-    key_weight_grad, value_weight_grad, next_hidden, prev_grad = call(
+    key_weight_grad, value_weight_grad, prev_grad, next_hidden = call(
         sum_kernel,
         [((HALF, KVW), BF16)] * 2 + [(wide, BF16)] * 2,
         [VMEM((HALF, KVW), BF16)] * 2 + [dma((4,))],
@@ -304,7 +304,7 @@
         [spec(SMEM)] + [spec(VMEM)] * 2 + [spec(ANY)] * 2,
         [spec(ANY)] * 4,
         16,
-    )(core.reshape(1), mine, both, next_hidden, prev_grad)
+    )(core.reshape(1), mine, both, prev_grad, next_hidden)
     return (
         next_hidden[None, None],
         prev_grad[None, None],

time: 44.7 us -> 44.6 us (level)
  blocking collectives: 17.9 us -> 11.9 us
  waiting for transfers between devices: 5.04 us -> 9.96 us
  starting transfers between devices: 11.7 us -> 12.9 us
    all_gather x1, blocking collectives: 17.9 us -> 11.9 us  [per_device(): both = lax.all_gather(theirs, 'dp', axis=0, axis_index_groups=pairs)]
    all_to_all x1, waiting for transfers between devices: 5.04 us -> 9.95 us  [per_device(): lax.all_to_all(send, 'dp', 0, 0, tiled=True, axis_index_groups=same_core)]
    ppermute x2, starting transfers between devices: 5.65 us -> 6.79 us  [along(): return lax.ppermute(value, axis, pairs)]
where the time goes in v5:
time: 44.6 us; the launch traced here: 44.3 us
  starting transfers between devices  12.9 us (29%)
  blocking collectives  11.9 us (27%)
  waiting for transfers between devices  9.96 us (22%)
  Pallas kernels  8.85 us (20%)
  between operations  0.73 us (2%)
    all_gather x1, blocking collectives, per_device(): both = lax.all_gather(theirs, 'dp', axis=0, axis_index_groups=pairs)  11.9 us
    all_to_all x1, waiting for transfers between devices, per_device(): lax.all_to_all(send, 'dp', 0, 0, tiled=True, axis_index_groups=same_core)  9.95 us
    ppermute x2, starting transfers between devices, along(): return lax.ppermute(value, axis, pairs)  6.79 us
    pallas_call x1, Pallas kernels, section_call(): call(section_kernel, [((CHIPS, CH, ROWS + 2 * KVW), BF16), (wide, BF16),...  6.42 us
    all_to_all x1, starting transfers between devices, per_device(): lax.all_to_all(send, 'dp', 0, 0, tiled=True, axis_index_groups=same_core)  6.1 us
    pallas_call x1, Pallas kernels, per_device(): call(query_kernel, [(wide, BF16)], [], 100000000, [spec(VMEM)] * 2, [spec...  1.06 us
    pallas_call x1, Pallas kernels, per_device(): call(sum_kernel, [((HALF, KVW), BF16)] * 2 + [(wide, BF16)] * 2, [VMEM((H...  0.91 us
  transfers between devices with their start and end apart: 3, of which 1 were waited for; matrix products, arithmetic and copies ran while one was open for 0% of the time, Pallas kernels for 3%

profile of v5, /device:TPU:1, one launch (start us, length us, event | category | flops | bytes accessed | tf_op | source)
XLA Modules:
  0.0 44.3 jit_solution(7338922024474744122)
XLA Ops:
  0.6 6.4 %shard_map.153 = (bf16[8,64,1280]{2,1,0:T(8,128)(2,1)}, bf16[64,2048]{1,0:T(8,128)(2,1)}, bf16[64,2048]{1,0:T(8,128)(2,1)}, bf16[128,512]{1,0:T(8,128)(2,1)}, bf...) custom-call(s32[2]{0:T(128)} %bitcast.30, bf16[64,2048]{1,0:T(8,128)(2,1)} %bitcast.22, ...), custom_call_target="tpu_custom_call" | custom-call | flops 1600000000 | bytes 6291456 | tf_op jit(solution)/shard_map/pallas_call | solution.py:232
  7.1 0.0 copy-start.3
  7.1 0.0 copy-start.2
  7.1 0.0 copy-start
  7.1 0.0 copy-start.1
  7.1 6.1 %all-to-all-start = ((bf16[8,64,1280]{2,1,0:T(8,128)(2,1)}), bf16[8,64,1280]{2,1,0:T(8,128)(2,1)S(1)}, u32[]{:S(2)}, u32[]{:S(2)}) async-start(bf16[8,64,1280]{2,1,0:T(8,128)(2,1)} %get-tuple-element.20), calls=%async_computation | async-start | bytes 2621440 | tf_op jit(solution)/shard_map/all_to_all | solution.py:276
  13.2 0.0 copy-done.3
  13.2 1.3 %collective-permute-start = (bf16[64,2048]{1,0:T(8,128)(2,1)S(1)}, bf16[64,2048]{1,0:T(8,128)(2,1)S(1)}, u32[]{:S(2)}, u32[]{:S(2)}) collective-permute-start(bf16[64,2048]{1,0:T(8,128)(2,1)S(1)} %copy-done.3), channel_id=1, source_target_pairs={{16,0},{32,16},{48,32},{64,48},{80,64},{96,80},{112,96},{128,112},... | collective-permute-start | bytes 786440 | tf_op jit(solution)/shard_map/ppermute | solution.py:259
  14.5 0.0 copy-done.2
  14.5 5.5 %collective-permute-start.1 = (bf16[64,2048]{1,0:T(8,128)(2,1)S(1)}, bf16[64,2048]{1,0:T(8,128)(2,1)S(1)}, u32[]{:S(2)}, u32[]{:S(2)}) collective-permute-start(bf16[64,2048]{1,0:T(8,128)(2,1)S(1)} %copy-done.2), channel_id=1, source_target_pairs={{0,16},{16,32},{32,48},{48,64},{64,80},{80,96},{96,112},{112,128},... | collective-permute-start | bytes 786440 | tf_op jit(solution)/shard_map/ppermute | solution.py:259
  20.0 0.0 copy-done
  20.0 0.0 copy-done.1
  20.0 1.1 %shard_map.156 = bf16[64,2048]{1,0:T(8,128)(2,1)} custom-call(bf16[4,192,256]{2,1,0:T(8,128)(2,1)S(1)} %copy-done, bf16[192,512]{1,0:T(8,128)(2,1)S(1)} %copy-done.1), custom_call_target="tpu_custom_call" | custom-call | flops 100000000 | bytes 6291456 | tf_op jit(solution)/shard_map/pallas_call | solution.py:279
  21.1 10.0 %all-to-all-done.recv = bf16[8,64,1280]{2,1,0:T(8,128)(2,1)S(1)} async-done(((bf16[8,64,1280]{2,1,0:T(8,128)(2,1)}), bf16[8,64,1280]{2,1,0:T(8,128)(2,1)S(1)}, u32[]{:S(2)}, u32[]{:S(2)}) %all-to-all-start) | async-done | bytes 1310752 | tf_op jit(solution)/shard_map/all_to_all | solution.py:276
  31.1 0.5 %shard_map.154 = (f32[128,1024]{1,0:T(8,128)S(1)}, bf16[128,1024]{1,0:T(8,128)(2,1)S(1)}) custom-call(s32[1]{0:T(128)} %bitcast.core, bf16[8,64,1280]{2,1,0:T(8,128)(2,1)S(1)} %all-to-all-done.recv), custom_call_target="tpu_custom_call" | custom-call | flops 270000000 | bytes 6291456 | tf_op jit(solution)/shard_map/pallas_call | solution.py:289
  31.5 11.9 %all-gather = bf16[256,1024]{1,0:T(8,128)(2,1)S(1)} all-gather(bf16[128,1024]{1,0:T(8,128)(2,1)S(1)} %get-tuple-element.22), channel_id=2, replica_groups={{0,1},{2,3},{4,5},{6,7},{8,9},{10,11},{12,13},{14,15},{16,17},{18,19},{..., dimensions={0}, use_global_device_ids=true | all-gather | bytes 786432 | tf_op jit(solution)/shard_map/all_gather | solution.py:298
  43.4 0.0 collective-permute-done.back_in
  43.4 0.0 collective-permute-done.1.fwd_in
  43.4 0.9 %shard_map.155 = (bf16[128,512]{1,0:T(8,128)(2,1)}, bf16[128,512]{1,0:T(8,128)(2,1)}, bf16[64,2048]{1,0:T(8,128)(2,1)}, bf16[64,2048]{1,0:T(8,128)(2,1)}) custom-call(s32[1]{0:T(128)} %bitcast.core, f32[128,1024]{1,0:T(8,128)S(1)} %get-tuple-element.21.mine, bf16[2,128,1024]{2,1,0:T(8,128)(2,1)S(1)} %bitcast.19, ...), custom_call_target="tpu_custom_call" | custom-call | flops 1000000 | bytes 6291456 | tf_op jit(solution)/shard_map/pallas_call | solution.py:299
Async XLA Ops:
  7.1 6.1 %copy-start.3 = (bf16[64,2048]{1,0:T(8,128)(2,1)S(1)}, bf16[64,2048]{1,0:T(8,128)(2,1)}, u32[]{:S(2)}) copy-start(bf16[64,2048]{1,0:T(8,128)(2,1)} %get-tuple-element.23) | copy-start | bytes 786436
  7.1 7.4 %copy-start.2 = (bf16[64,2048]{1,0:T(8,128)(2,1)S(1)}, bf16[64,2048]{1,0:T(8,128)(2,1)}, u32[]{:S(2)}) copy-start(bf16[64,2048]{1,0:T(8,128)(2,1)} %get-tuple-element.24) | copy-start | bytes 786436
  7.1 12.9 %copy-start = (bf16[4,192,256]{2,1,0:T(8,128)(2,1)S(1)}, bf16[4,192,256]{2,1,0:T(8,128)(2,1)}, u32[]{:S(2)}) copy-start(bf16[4,192,256]{2,1,0:T(8,128)(2,1)} %get-tuple-element.27.gs) | copy-start | bytes 1179652
  7.1 12.9 %copy-start.1 = (bf16[192,512]{1,0:T(8,128)(2,1)S(1)}, bf16[192,512]{1,0:T(8,128)(2,1)}, u32[]{:S(2)}) copy-start(bf16[192,512]{1,0:T(8,128)(2,1)} %get-tuple-element.28.keys) | copy-start | bytes 589828
  7.1 23.9 %all-to-all-start = ((bf16[8,64,1280]{2,1,0:T(8,128)(2,1)}), bf16[8,64,1280]{2,1,0:T(8,128)(2,1)S(1)}, u32[]{:S(2)}, u32[]{:S(2)}) async-start(bf16[8,64,1280]{2,1,0:T(8,128)(2,1)} %get-tuple-element.20), calls=%async_computation | async-start | bytes 2621440 | tf_op jit(solution)/shard_map/all_to_all | solution.py:276
  13.2 30.2 %collective-permute-start = (bf16[64,2048]{1,0:T(8,128)(2,1)S(1)}, bf16[64,2048]{1,0:T(8,128)(2,1)S(1)}, u32[]{:S(2)}, u32[]{:S(2)}) collective-permute-start(bf16[64,2048]{1,0:T(8,128)(2,1)S(1)} %copy-done.3), channel_id=1, source_target_pairs={{16,0},{32,16},{48,32},{64,48},{80,64},{96,80},{112,96},{128,112},... | collective-permute-start | bytes 786440 | tf_op jit(solution)/shard_map/ppermute | solution.py:259
  14.5 28.9 %collective-permute-start.1 = (bf16[64,2048]{1,0:T(8,128)(2,1)S(1)}, bf16[64,2048]{1,0:T(8,128)(2,1)S(1)}, u32[]{:S(2)}, u32[]{:S(2)}) collective-permute-start(bf16[64,2048]{1,0:T(8,128)(2,1)S(1)} %copy-done.2), channel_id=1, source_target_pairs={{0,16},{16,32},{32,48},{48,64},{64,80},{80,96},{96,112},{112,128},... | collective-permute-start | bytes 786440 | tf_op jit(solution)/shard_map/ppermute | solution.py:259
